TPU v7x, 32 devices: a whole 2x2x4 slice. The times are simulated.
32 devices in a mesh: samp: 4 (over y, core), sp: 8 (over z, x).
Axes of the slice: x: 2, y: 2, z: 4, core: 2. Of those that a mesh axis runs over, the one named last changes fastest.
Arguments:
- tokens: bfloat16 [4, 96, 160, 768], P('samp', 'sp'), may hold values from -6 to 6
- cotangent: bfloat16 [4, 96, 160, 768], P('samp', 'sp'), may hold values from -6 to 6
- storm_weight: int32 [4], P('samp'), may hold values from 16 to 192
- filter_master: float32 [768, 384], P(('samp', 'sp')), may hold values from -0.4375 to 0.4375
- in_master: float32 [768, 3072], P(('samp', 'sp')), may hold values from -0.21875 to 0.21875
- out_master: float32 [3072, 768], P(('samp', 'sp')), may hold values from -0.109375 to 0.109375
- small_master: float32 [9984], P(('samp', 'sp')), may hold values from -1.2 to 1.6, as said below
- filter_m: float32 [768, 384], P(('samp', 'sp')), may hold values from -128 to 128
- filter_v: float32 [768, 384], P(('samp', 'sp')), may hold values from 1536 to 6144
- in_m: float32 [768, 3072], P(('samp', 'sp')), may hold values from -96 to 96
- in_v: float32 [768, 3072], P(('samp', 'sp')), may hold values from 921.6 to 3686.4
- out_m: float32 [3072, 768], P(('samp', 'sp')), may hold values from -192 to 192
- out_v: float32 [3072, 768], P(('samp', 'sp')), may hold values from 4300.8 to 17203.2
- small_m: float32 [9984], P(('samp', 'sp')), may hold values from -160 to 160
- small_v: float32 [9984], P(('samp', 'sp')), may hold values from 3072 to 12288
- filter_ema: float32 [768, 384], P(('samp', 'sp')), may hold values from -0.4375 to 0.4375
- in_ema: float32 [768, 3072], P(('samp', 'sp')), may hold values from -0.21875 to 0.21875
- out_ema: float32 [3072, 768], P(('samp', 'sp')), may hold values from -0.109375 to 0.109375
- small_ema: float32 [9984], P(('samp', 'sp')), may hold values from 0.5 to 1.5
Outputs:
- result: bfloat16 [4, 96, 160, 768], P('samp', 'sp')
- input_grad: float32 [4, 96, 160, 768], P('samp', 'sp')
- filter_grad: float32 [768, 384], P(('samp', 'sp'))
- in_grad: float32 [768, 3072], P(('samp', 'sp'))
- out_grad: float32 [3072, 768], P(('samp', 'sp'))
- small_grad: float32 [9984], P(('samp', 'sp'))
- filter_new: float32 [768, 384], P(('samp', 'sp'))
- in_new: float32 [768, 3072], P(('samp', 'sp'))
- out_new: float32 [3072, 768], P(('samp', 'sp'))
- small_new: float32 [9984], P(('samp', 'sp'))
- filter_m_new: float32 [768, 384], P(('samp', 'sp'))
- filter_v_new: float32 [768, 384], P(('samp', 'sp'))
- in_m_new: float32 [768, 3072], P(('samp', 'sp'))
- in_v_new: float32 [768, 3072], P(('samp', 'sp'))
- out_m_new: float32 [3072, 768], P(('samp', 'sp'))
- out_v_new: float32 [3072, 768], P(('samp', 'sp'))
- small_m_new: float32 [9984], P(('samp', 'sp'))
- small_v_new: float32 [9984], P(('samp', 'sp'))
- filter_ema_new: float32 [768, 384], P(('samp', 'sp'))
- in_ema_new: float32 [768, 3072], P(('samp', 'sp'))
- out_ema_new: float32 [3072, 768], P(('samp', 'sp'))
- small_ema_new: float32 [9984], P(('samp', 'sp'))
Inputs may be any that keep to these rules, and one draw needn't show every extreme that they name: `small_master`: rows 0 and 2 of the small vector are gains, the others biases.
All inputs are finite; a program needn't handle non-finite values.
Results may differ from a plain program's by a relative error of at most 0.014.
Values may be sent and summed in bfloat16 or wider, within the bound.
No kernel may reach another device: no remote copies, remote signals or barrier semaphores. Data moves between devices by JAX's collectives and lax.ppermute only.
A program may use at most 320 MiB of HBM per device.

v0:
```python
import math

import jax
import jax.numpy as jnp
from jax import lax
from jax.sharding import PartitionSpec as P

NB = 8
STEP = 10


HIGHEST = lax.Precision.HIGHEST
NORM_EPS = 1e-05
BETA_ONE = 0.9
BETA_TWO = 0.95
ADAM_EPS = 1e-08
DECAY = 0.05
EMA_KEEP = 0.75


def gelu_exact(values):
    return jax.nn.gelu(values, approximate=False)


def norm_forward(values):
    center = values - jnp.mean(values, axis=-1, keepdims=True)
    inv_std = lax.rsqrt(jnp.mean(center * center, axis=-1, keepdims=True) + NORM_EPS)
    return (center * inv_std, inv_std)


def norm_back(upstream, normed, inv_std, gain):
    scaled = upstream * gain
    first_mean = jnp.mean(scaled, axis=-1, keepdims=True)
    second_mean = jnp.mean(scaled * normed, axis=-1, keepdims=True)
    leading = tuple(range(upstream.ndim - 1))
    input_part = inv_std * (scaled - first_mean - normed * second_mean)
    return (input_part, jnp.sum(upstream * normed, axis=leading), jnp.sum(upstream, axis=leading))


def dft_table(points):
    positions = jnp.arange(points, dtype=jnp.int32)
    phases = positions[:, None] * positions[None, :] % points
    angles = phases.astype(jnp.float32) * (2.0 * math.pi / points)
    factor = 1.0 / math.sqrt(points)
    return (jnp.cos(angles) * factor, jnp.sin(angles) * factor)


def lat_table(cosine, sine_part, sign_value):
    upper_rows = jnp.stack([cosine, -sign_value * sine_part], axis=-1)
    lower_rows = jnp.stack([sign_value * sine_part, cosine], axis=-1)
    return jnp.stack([upper_rows, lower_rows], axis=1)


def split_table(table):
    upper_part = table.astype(jnp.bfloat16)
    lower_part = (table - upper_part.astype(jnp.float32)).astype(jnp.bfloat16)
    return (upper_part, lower_part)


def table_first(form, table, values):
    upper_part, lower_part = split_table(table)
    return jnp.einsum(form, upper_part, values, preferred_element_type=jnp.float32) + jnp.einsum(
        form, lower_part, values, preferred_element_type=jnp.float32
    )


def table_second(form, values, table):
    upper_part, lower_part = split_table(table)
    return jnp.einsum(form, values, upper_part, preferred_element_type=jnp.float32) + jnp.einsum(
        form, values, lower_part, preferred_element_type=jnp.float32
    )


def complex_mix(inputs, weight):
    shape_in = inputs.shape
    size_block = weight.shape[1] // 2
    grouped = inputs.reshape(shape_in[:4] + (NB, size_block))
    matrices = weight.reshape(NB, size_block, 2, size_block)
    product = jnp.einsum(
        "sgckbi,bieo->sgcekbo", grouped, matrices, preferred_element_type=jnp.float32
    )
    real_part = product[:, :, 0, 0] - product[:, :, 1, 1]
    imag_part = product[:, :, 1, 0] + product[:, :, 0, 1]
    return jnp.stack([real_part, imag_part], axis=2).reshape(shape_in)


def mix_back(upstream, inputs, weight):
    shape_in = inputs.shape
    size_block = weight.shape[1] // 2
    grouped = inputs.reshape(shape_in[:4] + (NB, size_block))
    upstream_grouped = upstream.reshape(shape_in[:4] + (NB, size_block))
    matrices = weight.reshape(NB, size_block, 2, size_block)
    toward = jnp.einsum(
        "sgekbo,bico->sgeckbi", upstream_grouped, matrices, preferred_element_type=jnp.float32
    )
    grad_real = toward[:, :, 0, 0] + toward[:, :, 1, 1]
    grad_imag = toward[:, :, 1, 0] - toward[:, :, 0, 1]
    grad_inputs = jnp.stack([grad_real, grad_imag], axis=2).reshape(shape_in)
    outer_sums = jnp.einsum(
        "sgckbi,sgekbo->cebio", grouped, upstream_grouped, preferred_element_type=jnp.float32
    )
    weight_real = outer_sums[0, 0] + outer_sums[1, 1]
    weight_imag = outer_sums[0, 1] - outer_sums[1, 0]
    weight_grad = jnp.stack([weight_real, weight_imag], axis=2).reshape(weight.shape)
    bias_grad = jnp.sum(upstream, axis=(0, 1, 3), dtype=jnp.float32)
    return (grad_inputs, weight_grad, bias_grad)


def adam_update(master, gradient, moment, second, average, step_rate):
    moment_new = BETA_ONE * moment + (1.0 - BETA_ONE) * gradient
    second_new = BETA_TWO * second + (1.0 - BETA_TWO) * gradient * gradient
    scaled_moment = moment_new / (1.0 - BETA_ONE**STEP)
    scaled_second = second_new / (1.0 - BETA_TWO**STEP)
    master_new = master - step_rate * (
        scaled_moment / (jnp.sqrt(scaled_second) + ADAM_EPS) + DECAY * master
    )
    average_new = EMA_KEEP * average + (1.0 - EMA_KEEP) * master_new
    return (master_new, moment_new, second_new, average_new)


def shards(
    tokens,
    cotangent,
    storm_weight,
    filter_master,
    in_master,
    out_master,
    small_master,
    filter_m,
    filter_v,
    in_m,
    in_v,
    out_m,
    out_v,
    small_m,
    small_v,
    filter_ema,
    in_ema,
    out_ema,
    small_ema,
):
    filter_work, small_work = (
        lax.all_gather(filter_master.astype(jnp.bfloat16), ("samp", "sp"), axis=0, tiled=True),
        lax.all_gather(small_master.astype(jnp.bfloat16), ("samp", "sp"), axis=0, tiled=True),
    )
    width = filter_work.shape[0]
    size_block = width // NB
    params = small_work.astype(jnp.float32).reshape(13, width)
    inputs = tokens.astype(jnp.float32)
    normed_one, inv_one = norm_forward(inputs)
    first = normed_one * params[0] + params[1]
    lon_cos, lon_sin = dft_table(tokens.shape[2])
    lon_forward = jnp.stack([lon_cos, -lon_sin], axis=1)
    lon_inverse = jnp.stack([lon_cos, -lon_sin], axis=0)
    spectrum = jnp.einsum("shwd,wck->shckd", first, lon_forward, precision=HIGHEST).astype(
        jnp.bfloat16
    )
    arrived = lax.all_to_all(spectrum, "sp", split_axis=3, concat_axis=1, tiled=True)
    lat_cos, lat_sin = dft_table(arrived.shape[1])
    lat_forward = lat_table(lat_cos, lat_sin, -1.0)
    lat_inverse = lat_table(lat_cos, lat_sin, 1.0)
    modes = table_first("gohc,shckd->sgokd", lat_forward, arrived).astype(jnp.bfloat16)
    bias_one = params[4:6][:, None, :]
    bias_two = params[6:8][:, None, :]
    pre_one = complex_mix(modes, filter_work[:, : 2 * size_block]) + bias_one
    hidden_one = gelu_exact(pre_one).astype(jnp.bfloat16)
    pre_two = complex_mix(hidden_one, filter_work[:, 2 * size_block :]) + bias_two
    leaving = jnp.einsum("gohc,shckd->sgokd", lat_inverse, pre_two, precision=HIGHEST).astype(
        jnp.bfloat16
    )
    returned = lax.all_to_all(leaving, "sp", split_axis=1, concat_axis=3, tiled=True)
    spatial = table_second("shckd,ckw->shwd", returned, lon_inverse)
    mixed = spatial + first + inputs
    in_work, out_work = (
        lax.all_gather(in_master.astype(jnp.bfloat16), ("samp", "sp"), axis=0, tiled=True),
        lax.all_gather(out_master.astype(jnp.bfloat16), ("samp", "sp"), axis=0, tiled=True),
    )
    normed_two, inv_two = norm_forward(mixed)
    second = (normed_two * params[2] + params[3]).astype(jnp.bfloat16).reshape(-1, width)
    pre_dense = jnp.dot(second, in_work, preferred_element_type=jnp.float32) + params[9:13].reshape(
        -1
    )
    act_dense = gelu_exact(pre_dense).astype(jnp.bfloat16)
    branch = jnp.dot(act_dense, out_work, preferred_element_type=jnp.float32) + params[8]
    result = (mixed + branch.reshape(mixed.shape)).astype(jnp.bfloat16)
    filter_back = lax.all_gather(
        filter_master.astype(jnp.bfloat16), ("samp", "sp"), axis=0, tiled=True
    )
    in_back, out_back = (
        lax.all_gather(in_master.astype(jnp.bfloat16), ("samp", "sp"), axis=0, tiled=True),
        lax.all_gather(out_master.astype(jnp.bfloat16), ("samp", "sp"), axis=0, tiled=True),
    )
    sample_scale = storm_weight.astype(jnp.float32)[:, None, None, None] / 64.0
    grad_out = cotangent.astype(jnp.float32) * sample_scale
    grad_low = grad_out.astype(jnp.bfloat16).reshape(-1, width)
    out_local = jnp.einsum("tf,td->fd", act_dense, grad_low, preferred_element_type=jnp.float32)
    out_bias_grad = jnp.sum(grad_low, axis=0, dtype=jnp.float32)
    grad_act = jnp.einsum("td,fd->tf", grad_low, out_back, preferred_element_type=jnp.float32)
    dense_values, dense_pull = jax.vjp(gelu_exact, pre_dense)
    grad_pre = dense_pull(grad_act)[0].astype(jnp.bfloat16)
    in_local = jnp.einsum("td,tf->df", second, grad_pre, preferred_element_type=jnp.float32)
    in_bias_grad = jnp.sum(grad_pre, axis=0, dtype=jnp.float32)
    grad_second = jnp.einsum(
        "tf,df->td", grad_pre, in_back, preferred_element_type=jnp.float32
    ).reshape(mixed.shape)
    grad_norm_two, gain_two_grad, shift_two_grad = norm_back(
        grad_second, normed_two, inv_two, params[2]
    )
    grad_mixed = grad_out + grad_norm_two
    grad_leaving = jnp.einsum("shwd,ckw->shckd", grad_mixed, lon_inverse, precision=HIGHEST).astype(
        jnp.bfloat16
    )
    grad_arrived = lax.all_to_all(grad_leaving, "sp", split_axis=3, concat_axis=1, tiled=True)
    grad_pre_two = table_first("gohc,sgokd->shckd", lat_inverse, grad_arrived).astype(jnp.bfloat16)
    grad_hidden, weight_two_grad, bias_two_grad = mix_back(
        grad_pre_two, hidden_one, filter_back[:, 2 * size_block :]
    )
    gelu_values, gelu_pull = jax.vjp(gelu_exact, pre_one)
    grad_pre_one = gelu_pull(grad_hidden)[0].astype(jnp.bfloat16)
    grad_modes, weight_one_grad, bias_one_grad = mix_back(
        grad_pre_one, modes, filter_back[:, : 2 * size_block]
    )
    grad_spectrum = jnp.einsum(
        "gohc,sgokd->shckd", lat_forward, grad_modes, precision=HIGHEST
    ).astype(jnp.bfloat16)
    grad_sent = lax.all_to_all(grad_spectrum, "sp", split_axis=1, concat_axis=3, tiled=True)
    grad_first = grad_mixed + table_second("shckd,wck->shwd", grad_sent, lon_forward)
    grad_norm_one, gain_one_grad, shift_one_grad = norm_back(
        grad_first, normed_one, inv_one, params[0]
    )
    input_grad = grad_mixed + grad_norm_one
    norm_rows = jnp.stack([gain_one_grad, shift_one_grad, gain_two_grad, shift_two_grad])
    small_local = jnp.concatenate(
        [
            norm_rows,
            bias_one_grad,
            bias_two_grad,
            out_bias_grad[None, :],
            in_bias_grad.reshape(-1, width),
        ],
        axis=0,
    ).reshape(-1)
    filter_local = jnp.concatenate([weight_one_grad, weight_two_grad], axis=1)
    filter_grad, in_grad, out_grad, small_grad = (
        lax.psum_scatter(filter_local, ("samp", "sp"), scatter_dimension=0, tiled=True),
        lax.psum_scatter(in_local, ("samp", "sp"), scatter_dimension=0, tiled=True),
        lax.psum_scatter(out_local, ("samp", "sp"), scatter_dimension=0, tiled=True),
        lax.psum_scatter(small_local, ("samp", "sp"), scatter_dimension=0, tiled=True),
    )
    filter_new, filter_m_new, filter_v_new, filter_ema_new = adam_update(
        filter_master, filter_grad, filter_m, filter_v, filter_ema, 0.2
    )
    in_new, in_m_new, in_v_new, in_ema_new = adam_update(
        in_master, in_grad, in_m, in_v, in_ema, 0.1
    )
    out_new, out_m_new, out_v_new, out_ema_new = adam_update(
        out_master, out_grad, out_m, out_v, out_ema, 0.05
    )
    small_new, small_m_new, small_v_new, small_ema_new = adam_update(
        small_master, small_grad, small_m, small_v, small_ema, 0.5
    )
    return (
        result,
        input_grad,
        filter_grad,
        in_grad,
        out_grad,
        small_grad,
        filter_new,
        in_new,
        out_new,
        small_new,
        filter_m_new,
        filter_v_new,
        in_m_new,
        in_v_new,
        out_m_new,
        out_v_new,
        small_m_new,
        small_v_new,
        filter_ema_new,
        in_ema_new,
        out_ema_new,
        small_ema_new,
    )


def solution(mesh):
    return jax.shard_map(
        shards,
        mesh=mesh,
        in_specs=(
            P("samp", "sp", None, None),
            P("samp", "sp", None, None),
            P("samp"),
            P(("samp", "sp"), None),
            P(("samp", "sp"), None),
            P(("samp", "sp"), None),
            P(("samp", "sp")),
            P(("samp", "sp"), None),
            P(("samp", "sp"), None),
            P(("samp", "sp"), None),
            P(("samp", "sp"), None),
            P(("samp", "sp"), None),
            P(("samp", "sp"), None),
            P(("samp", "sp")),
            P(("samp", "sp")),
            P(("samp", "sp"), None),
            P(("samp", "sp"), None),
            P(("samp", "sp"), None),
            P(("samp", "sp")),
        ),
        out_specs=(
            P("samp", "sp", None, None),
            P("samp", "sp", None, None),
            P(("samp", "sp"), None),
            P(("samp", "sp"), None),
            P(("samp", "sp"), None),
            P(("samp", "sp")),
            P(("samp", "sp"), None),
            P(("samp", "sp"), None),
            P(("samp", "sp"), None),
            P(("samp", "sp")),
            P(("samp", "sp"), None),
            P(("samp", "sp"), None),
            P(("samp", "sp"), None),
            P(("samp", "sp"), None),
            P(("samp", "sp"), None),
            P(("samp", "sp"), None),
            P(("samp", "sp")),
            P(("samp", "sp")),
            P(("samp", "sp"), None),
            P(("samp", "sp"), None),
            P(("samp", "sp"), None),
            P(("samp", "sp")),
        ),
        check_vma=False,
    )
```

profile of v0, /device:TPU:0, one launch (start us, length us, event | category | flops | bytes accessed | tf_op | source)
XLA Modules:
  0.0 1699.0 jit_solution(9117439085908961704)
XLA Ops:
  14.2 42.2 %all-reduce = bf16[9984]{0:T(1024)(128)(2,1)S(1)} all-reduce(bf16[9984]{0:T(1024)(128)(2,1)S(1)} %dynamic-update-slice), channel_id=1, replica_groups=mesh['samp'=4,'sp'=8] {'samp','sp'}, use_global_device_ids=true, to_apply=%add | all-reduce | flops 9984 | bytes 39936
  69.3 18.7 %copy.266 = bf16[1,12,2,160,768]{4,2,1,0,3:T(2,128)(2,1)} copy(bf16[1,12,2,160,768]{4,3,1,2,0:T(8,128)(2,1)S(1)} %convert_bitcast_fusion.1) | data formatting | bytes 11796480 | tf_op jit(solution)/shard_map/convert_element_type | solution.py:155
  93.4 187.2 %all_gather.16 = bf16[768,384]{1,0:T(8,128)(2,1)S(1)} all-gather(bf16[24,384]{1,0:T(8,128)(2,1)S(1)} %convert_element_type.257), channel_id=1, replica_groups=mesh['samp'=4,'sp'=8] {'samp','sp'}, dimensions={0}, use_global_device_ids=true | all-gather | bytes 608256 | tf_op jit(solution)/shard_map/all_gather | solution.py:143
  307.6 14.3 reshape.1335
  322.0 17.8 %convolution_bitcast_fusion.3 = f32[1,96,2,2,20,8,96]{6,1,3,4,2,5,0:T(8,128)} fusion(bf16[8,96,2,96,1,1]{3,1,2,5,4,0:T(8,128)(2,1)S(1)} %copy.333, bf16[96,2,20,8,96,1]{4,3,0,1,2,5:T(8,128)(2,1)} %bitcast.367), kind=kOutput, calls=%fused_computation.41 | convolution fusion | flops 1132462080 | bytes 29786112 | tf_op jit(solution)/shard_map/sgckbi,bieo->sgcekbo/dot_general | solution.py:79
  347.1 13.2 fusion.213
  360.3 37.8 %fusion.34 = (bf16[96,2,20,8,96,1]{4,0,2,3,1,5:T(8,128)(2,1)}, f32[96,2,20,8,96]{4,0,2,3,1:T(8,128)}) fusion(f32[96,1,20,8,96]{4,0,2,3,1:T(8,128)S(1)} %fusion.214, f32[96,1,20,8,96]{4,0,2,3,1:T(8,128)} %fusion.213, f32[2,8,96]{2,1,0:T(8,128)S(1)} %slice.146), kind=kLoop, calls=%fused_computation.83 | loop fusion | flops 197591040 | bytes 29497344 | tf_op jit(solution)/shard_map/convert_element_type | solution.py:166
  398.1 14.6 convolution_bitcast_fusion.2
  412.7 15.6 slice_subtract_fusion.2
  468.6 13.8 fusion.65
  482.5 15.0 copy.282
  507.5 130.6 %all-to-all-done.1 = bf16[1,96,2,20,768]{4,2,3,0,1:T(2,128)(2,1)} async-done(((bf16[1,96,2,20,768]{4,2,3,0,1:T(2,128)(2,1)}), bf16[1,96,2,20,768]{4,2,3,0,1:T(2,128)(2,1)}, u32[]{:S(2)}, u32[]{:S(2)}) %all-to-all-start.1) | async-done | bytes 5898272 | tf_op jit(solution)/shard_map/all_to_all | solution.py:171
  660.7 60.1 %multiply_convert_fusion = (bf16[1920,3072]{1,0:T(8,128)(2,1)S(1)}, f32[1920,3072]{1,0:T(8,128)}, f32[1920,3072]{1,0:T(8,128)}) fusion(f32[3072]{0:T(1024)S(1)} %slice.191, bf16[1920,768]{1,0:T(8,128)(2,1)S(1)} %bitcast.388, bf16[768,3072]{1,0:T(8,128)(2,1)} %all-gather.3.cloned.1.call-done), kind=kOutput, calls=%fused_computation.4 | convolution fusion | flops 9448980480 | bytes 66662400 | tf_op jit(solution)/shard_map/dot_general | solution.py:180
  738.3 134.4 %reduce-scatter.6.cloned.1.call-done = f32[96,768]{1,0:T(8,128)} async-done(((f32[3072,768]{1,0:T(8,128)}), f32[96,768]{1,0:T(8,128)}) %reduce-scatter.6.cloned.1.call-update) | async-done | bytes 294928 | tf_op jit(solution)/shard_map/reduce_scatter | solution.py:247
  875.1 64.3 %all-gather.5.cloned.1.call-done = bf16[3072,768]{1,0:T(8,128)(2,1)} async-done(((bf16[96,768]{1,0:T(8,128)(2,1)}), bf16[3072,768]{1,0:T(8,128)(2,1)}) %all-gather.5.cloned.1.call-update) | async-done | bytes 4718608 | tf_op jit(solution)/shard_map/all_gather | solution.py:176
  939.4 26.6 %convert_reduce_fusion = (f32[3072]{0:T(1024)}, bf16[1920,3072]{1,0:T(8,128)(2,1)}) fusion(f32[1920,3072]{1,0:T(8,128)} %get-tuple-element.138, bf16[1920,768]{1,0:T(8,128)(2,1)S(1)} %bitcast.391, bf16[3072,768]{1,0:T(8,128)(2,1)} %all-gather.5.cloned.1.call-done, f32[1920,3072]{1,0:T(8,128)} %get-tuple-element.167, f32[3072]{0:T(1024)S(1)} %slice.191), kind=kOutput, calls=%fused_computation.2 | convolution fusion | flops 9159963648 | bytes 66674688 | tf_op jit(solution)/shard_map/td,fd->tf/dot_general | solution.py:198
  966.0 15.4 fusion.185
  988.2 13.7 convolution_add_fusion
  1016.0 30.8 %copy.287 = bf16[1,12,2,160,768]{4,2,1,0,3:T(2,128)(2,1)S(1)} copy(bf16[1,12,2,160,768]{4,3,1,2,0:T(8,128)(2,1)S(1)} %convert_bitcast_fusion) | data formatting | bytes 11796480 | tf_op jit(solution)/shard_map/convert_element_type | solution.py:210
  1046.8 134.5 %all_to_all.60 = bf16[1,12,2,160,768]{4,2,1,0,3:T(2,128)(2,1)S(1)} all-to-all(bf16[1,12,2,160,768]{4,2,1,0,3:T(2,128)(2,1)S(1)} %copy.287), channel_id=1, replica_groups=mesh['samp'=4,'sp'=8] {'sp'}, dimensions={3} | all-to-all | bytes 11796480 | tf_op jit(solution)/shard_map/all_to_all | solution.py:213
  1207.8 14.3 reshape.1345
  1230.6 17.8 %convolution_bitcast_fusion = f32[1,96,2,2,20,8,96]{6,1,4,5,3,2,0:T(8,128)} fusion(bf16[96,2,20,8,96,1]{4,3,0,1,2,5:T(8,128)(2,1)} %bitcast.366, bf16[8,96,2,96,1,1]{1,0,3,2,5,4:T(8,128)(2,1)S(1)} %bitcast.387), kind=kOutput, calls=%fused_computation.38 | convolution fusion | flops 1132462080 | bytes 29786112 | tf_op jit(solution)/shard_map/sgekbo,bico->sgeckbi/dot_general | solution.py:93
  1248.4 15.2 slice_add_fusion.1
  1266.7 17.6 %fusion.46 = bf16[96,2,20,8,96,1]{4,0,2,3,1,5:T(8,128)(2,1)} fusion(f32[96,2,20,8,96]{4,0,2,3,1:T(8,128)} %get-tuple-element.140, f32[96,1,20,8,96]{4,0,2,3,1:T(8,128)S(1)} %bitcast.361, f32[96,1,20,8,96]{4,0,2,3,1:T(8,128)} %bitcast.362, f32[2,8,96]{2,1,0:T(8,128)S(1)} %copy-done.52, f32[96,1,20,8,96]{4,0,2,3,1:T(8,128)} %copy-done.3, ...), kind=kLoop, calls=%fused_computation.104 | loop fusion | flops 50135040 | bytes 41293824 | tf_op jit(solution)/shard_map/convert_element_type | solution.py:219
  1295.9 16.1 fusion.197
  1312.1 14.7 convolution_bitcast_fusion.1
  1326.8 15.7 slice_add_fusion
  1383.0 14.2 fusion.67
  1397.2 14.6 copy.303
  1522.4 28.3 %convert_reduce_fusion.2 = f32[2,768]{1,0:T(2,128)S(1)} fusion(f32[1,96,2,20,768]{4,1,3,2,0:T(8,128)S(1)} %constant_dynamic-update-slice_fusion, f32[2,768]{1,0:T(2,128)S(1)} %slice.174, f32[1,96,1,20,768]{4,1,3,2,0:T(8,128)S(1)} %bitcast.376, f32[1,96,1,20,768]{4,1,3,2,0:T(8,128)S(1)} %bitcast.374), kind=kLoop, calls=%fused_computation.64 | loop fusion | flops 224131584 | bytes 23605248 | tf_op jit(solution)/shard_map/reduce_sum | solution.py:105
  1552.7 75.6 %reduce-scatter.4.cloned.1.call-done = f32[24,3072]{1,0:T(8,128)} async-done(((f32[768,3072]{1,0:T(8,128)}), f32[24,3072]{1,0:T(8,128)}) %reduce-scatter.4.cloned.1.call-update) | async-done | bytes 294928 | tf_op jit(solution)/shard_map/reduce_scatter | solution.py:246
  1644.4 40.0 %all-reduce.2 = f32[9984]{0:T(1024)S(1)} all-reduce(f32[9984]{0:T(1024)S(1)} %reshape.1351), channel_id=5, replica_groups=mesh['samp'=4,'sp'=8] {'samp','sp'}, use_global_device_ids=true, to_apply=%region_19.20.clone | all-reduce | flops 9984 | bytes 79872
  (292 shorter events, 398.0 us)
Async XLA Ops:
  7.9 80.1 %copy-start.31 = (f32[160,1,160]{0,2,1:T(8,128)}, f32[160,1,160]{0,2,1:T(8,128)S(1)}, u32[]{:S(2)}) copy-start(f32[160,1,160]{0,2,1:T(8,128)S(1)} %get-tuple-element.174) | copy-start | bytes 307204
  7.9 80.1 %copy-start.33 = (f32[160,1,160]{0,2,1:T(8,128)}, f32[160,1,160]{0,2,1:T(8,128)S(1)}, u32[]{:S(2)}) copy-start(f32[160,1,160]{0,2,1:T(8,128)S(1)} %get-tuple-element.175) | copy-start | bytes 307204
  11.0 634.5 %copy-start.47 = (f32[12,160]{1,0:T(8,128)}, f32[12,160]{1,0:T(8,128)S(1)}, u32[]{:S(2)}) copy-start(f32[12,160]{1,0:T(8,128)S(1)} %broadcast_multiply_fusion.4) | copy-start | bytes 23044
  13.9 631.6 %copy-start.55 = (f32[12,160]{1,0:T(8,128)}, f32[12,160]{1,0:T(8,128)S(1)}, u32[]{:S(2)}) copy-start(f32[12,160]{1,0:T(8,128)S(1)} %add_rsqrt_fusion.1) | copy-start | bytes 23044
  57.0 588.6 %copy-start.63 = (f32[768]{0:T(1024)}, f32[768]{0:T(1024)S(1)}, u32[]{:S(2)}) copy-start(f32[768]{0:T(1024)S(1)} %get-tuple-element.161) | copy-start | bytes 9220
  57.0 593.0 %copy-start.53 = (f32[768]{0:T(1024)}, f32[768]{0:T(1024)S(1)}, u32[]{:S(2)}) copy-start(f32[768]{0:T(1024)S(1)} %get-tuple-element.159) | copy-start | bytes 9220
  88.0 195.0 %all-to-all-start = ((bf16[1,12,2,160,768]{4,2,1,0,3:T(2,128)(2,1)}), bf16[1,12,2,160,768]{4,2,1,0,3:T(2,128)(2,1)}, u32[]{:S(2)}, u32[]{:S(2)}) async-start(bf16[1,12,2,160,768]{4,2,1,0,3:T(2,128)(2,1)} %copy.266), calls=%async_computation | async-start | bytes 11796480 | tf_op jit(solution)/shard_map/all_to_all | solution.py:158
  93.3 201.9 %copy-start.49 = (f32[1536]{0:T(1024)}, f32[1536]{0:T(1024)S(1)}, u32[]{:S(2)}) copy-start(f32[1536]{0:T(1024)S(1)} %get-tuple-element.164) | copy-start | bytes 18436
  93.4 266.9 %copy-start.51 = (f32[2,8,96]{2,1,0:T(8,128)}, f32[2,8,96]{2,1,0:T(8,128)S(1)}, u32[]{:S(2)}) copy-start(f32[2,8,96]{2,1,0:T(8,128)S(1)} %slice.146) | copy-start | bytes 18436
  281.5 116.6 %copy-start.10 = (bf16[8,96,2,96]{1,0,3,2:T(8,128)(2,1)}, bf16[8,96,2,96]{1,0,3,2:T(8,128)(2,1)S(1)}, u32[]{:S(2)}) copy-start(bf16[8,96,2,96]{1,0,3,2:T(8,128)(2,1)S(1)} %reshape.1337) | copy-start | bytes 884740
  282.9 185.7 %copy-start.27 = (f32[96,1,96,2]{2,0,3,1:T(8,128)}, f32[96,1,96,2]{2,0,3,1:T(8,128)S(1)}, u32[]{:S(2)}) copy-start(f32[96,1,96,2]{2,0,3,1:T(8,128)S(1)} %get-tuple-element.152) | copy-start | bytes 221188
  282.9 185.7 %copy-start.29 = (f32[96,1,96,2]{2,0,3,1:T(8,128)}, f32[96,1,96,2]{2,0,3,1:T(8,128)S(1)}, u32[]{:S(2)}) copy-start(f32[96,1,96,2]{2,0,3,1:T(8,128)S(1)} %get-tuple-element.157) | copy-start | bytes 221188
  497.5 140.6 %all-to-all-start.1 = ((bf16[1,96,2,20,768]{4,2,3,0,1:T(2,128)(2,1)}), bf16[1,96,2,20,768]{4,2,3,0,1:T(2,128)(2,1)}, u32[]{:S(2)}, u32[]{:S(2)}) async-start(bf16[1,96,2,20,768]{4,2,3,0,1:T(2,128)(2,1)} %copy.282), calls=%async_computation.1 | async-start | bytes 11796480 | tf_op jit(solution)/shard_map/all_to_all | solution.py:171
  502.2 158.5 %all-gather.3.cloned.1.call-start = ((), (), s32[]{:S(2)}) async-start(), calls=%async_computation.6 | async-start | bytes 4866048 | tf_op jit(solution)/shard_map/all_gather | solution.py:175
  503.0 369.7 %reduce-scatter.6.cloned.1.call-start = ((), (), s32[]{:S(2)}) async-start(), calls=%async_computation.9 | async-start | bytes 9732096 | tf_op jit(solution)/shard_map/reduce_scatter | solution.py:247
  504.4 141.2 %copy-start.17 = (f32[1,160,160]{1,2,0:T(8,128)}, f32[1,160,160]{1,2,0:T(8,128)S(1)}, u32[]{:S(2)}) copy-start(f32[1,160,160]{1,2,0:T(8,128)S(1)} %get-tuple-element.178) | copy-start | bytes 307204
  504.4 141.2 %copy-start.19 = (f32[1,160,160]{1,2,0:T(8,128)}, f32[1,160,160]{1,2,0:T(8,128)S(1)}, u32[]{:S(2)}) copy-start(f32[1,160,160]{1,2,0:T(8,128)S(1)} %get-tuple-element.179) | copy-start | bytes 307204
  652.8 68.1 %copy-start.14 = (bf16[1,12,160,768]{3,2,1,0:T(8,128)(2,1)}, bf16[1,12,160,768]{3,2,1,0:T(8,128)(2,1)S(1)}, u32[]{:S(2)}) copy-start(bf16[1,12,160,768]{3,2,1,0:T(8,128)(2,1)S(1)} %add_convert_fusion.3) | copy-start | bytes 8847364
  725.1 147.6 %copy-start.37 = (f32[96,768]{1,0:T(8,128)S(1)}, f32[96,768]{1,0:T(8,128)}, u32[]{:S(2)}) copy-start(f32[96,768]{1,0:T(8,128)} %param.36) | copy-start | bytes 884740
  725.1 147.6 %copy-start.38 = (f32[96,768]{1,0:T(8,128)S(1)}, f32[96,768]{1,0:T(8,128)}, u32[]{:S(2)}) copy-start(f32[96,768]{1,0:T(8,128)} %param.24) | copy-start | bytes 884740
  738.2 201.2 %copy-start.16 = (bf16[1,12,160,768]{3,2,1,0:T(8,128)(2,1)S(1)}, bf16[1,12,160,768]{3,2,1,0:T(8,128)(2,1)}, u32[]{:S(2)}) copy-start(bf16[1,12,160,768]{3,2,1,0:T(8,128)(2,1)} %get-tuple-element.136) | copy-start | bytes 8847364
  738.2 201.2 %all-gather.5.cloned.1.call-start = ((), (), s32[]{:S(2)}) async-start(), calls=%async_computation.7 | async-start | bytes 4866048 | tf_op jit(solution)/shard_map/all_gather | solution.py:176
  875.1 675.6 %all-reduce.5.cloned.1.call-start = ((), (), s32[]{:S(2)}) async-start(), calls=%async_computation.10 | async-start | bytes 2359296
  1295.9 332.4 %reduce-scatter.4.cloned.1.call-start = ((), (), s32[]{:S(2)}) async-start(), calls=%async_computation.8 | async-start | bytes 9732096 | tf_op jit(solution)/shard_map/reduce_scatter | solution.py:246
  1411.9 218.5 %all-to-all-start.3 = ((bf16[1,96,2,20,768]{4,2,3,0,1:T(2,128)(2,1)}), bf16[1,96,2,20,768]{4,2,3,0,1:T(2,128)(2,1)}, u32[]{:S(2)}, u32[]{:S(2)}) async-start(bf16[1,96,2,20,768]{4,2,3,0,1:T(2,128)(2,1)} %copy.303), calls=%async_computation.3 | async-start | bytes 11796480 | tf_op jit(solution)/shard_map/all_to_all | solution.py:226
  1522.3 106.0 %copy-start.22 = (f32[24,3072]{1,0:T(8,128)S(1)}, f32[24,3072]{1,0:T(8,128)}, u32[]{:S(2)}) copy-start(f32[24,3072]{1,0:T(8,128)} %param.23) | copy-start | bytes 884740
  1522.3 106.0 %copy-start.39 = (f32[24,3072]{1,0:T(8,128)S(1)}, f32[24,3072]{1,0:T(8,128)}, u32[]{:S(2)}) copy-start(f32[24,3072]{1,0:T(8,128)} %param.35) | copy-start | bytes 884740
  1522.3 105.9 %copy-start.40 = (f32[24,3072]{1,0:T(8,128)S(1)}, f32[24,3072]{1,0:T(8,128)}, u32[]{:S(2)}) copy-start(f32[24,3072]{1,0:T(8,128)} %param.28) | copy-start | bytes 884740
  1522.4 105.9 %copy-start.41 = (f32[24,3072]{1,0:T(8,128)S(1)}, f32[24,3072]{1,0:T(8,128)}, u32[]{:S(2)}) copy-start(f32[24,3072]{1,0:T(8,128)} %param.29) | copy-start | bytes 884740
  1550.6 86.1 %copy-start.32 = (f32[160,1,160]{0,2,1:T(8,128)S(1)}, f32[160,1,160]{0,2,1:T(8,128)}, u32[]{:S(2)}) copy-start(f32[160,1,160]{0,2,1:T(8,128)} %copy-done.31) | copy-start | bytes 307204
  1550.7 86.1 %copy-start.34 = (f32[160,1,160]{0,2,1:T(8,128)S(1)}, f32[160,1,160]{0,2,1:T(8,128)}, u32[]{:S(2)}) copy-start(f32[160,1,160]{0,2,1:T(8,128)} %copy-done.33) | copy-start | bytes 307204
  1552.0 86.5 %copy-start.44 = (f32[24,384]{1,0:T(8,128)}, f32[24,384]{1,0:T(8,128)S(1)}, u32[]{:S(2)}) copy-start(f32[24,384]{1,0:T(8,128)S(1)} %copy.326) | copy-start | bytes 110596
  (59 other events, 1026.1 us)
Sparse Core Ops, SparseCore 0:
  506.6 154.0 all-gather.2
  738.4 134.2 reduce-scatter.5
  876.7 62.6 all-gather.4
  1295.9 129.3 all-reduce.4
  1431.6 196.6 reduce-scatter.3
where the time goes:
time: 1710 us; the launch traced here: 1700 us
  waiting for transfers between devices  413 us (24%)
  blocking collectives  404 us (24%)
  local copies, waits for them, and re-layouts  336 us (20%)
  matrix products  311 us (18%)
  other arithmetic  203 us (12%)
    all_gather x1, blocking collectives, shards(): lax.all_gather(filter_master.astype(jnp.bfloat16), ('samp', 'sp'), axis=0...  187 us
    all_to_all x1, blocking collectives, shards(): lax.all_to_all(grad_leaving, 'sp', split_axis=3, concat_axis=1, tiled=True)  135 us
    reduce_scatter x1, waiting for transfers between devices, shards(): lax.psum_scatter(out_local, ('samp', 'sp'), scatter_dimension=0, tiled=True)  134 us
    all_to_all x1, waiting for transfers between devices, shards(): lax.all_to_all(leaving, 'sp', split_axis=1, concat_axis=3, tiled=True)  131 us
    unnamed x2, blocking collectives  82.2 us
    reduce_scatter x1, waiting for transfers between devices, shards(): lax.psum_scatter(in_local, ('samp', 'sp'), scatter_dimension=0, tiled=True)  75.6 us
    all_gather x1, waiting for transfers between devices, shards(): lax.all_gather(out_master.astype(jnp.bfloat16), ('samp', 'sp'), axis=0, t...  64.3 us
    dot_general x1, matrix products, shards(): jnp.dot(second, in_work, preferred_element_type=jnp.float32)  60.1 us
  transfers between devices with their start and end apart: 8, of which 5 were waited for; matrix products, arithmetic and copies ran while one was open for 16% of the time, Pallas kernels for 0%

commit v1 on v0

--- a/solution.py
+++ b/solution.py
@@ -1,8 +1,12 @@
+import functools
 import math
 
 import jax
 import jax.numpy as jnp
+import numpy as np
 from jax import lax
+from jax.experimental import pallas as pl
+from jax.experimental.pallas import tpu as pltpu
 from jax.sharding import PartitionSpec as P
 
 NB = 8
@@ -118,7 +122,7 @@
     return (master_new, moment_new, second_new, average_new)
 
 
-def shards(
+def plain_shards(
     tokens,
     cotangent,
     storm_weight,
@@ -285,9 +289,740 @@
     )
 
 
+F32 = jnp.float32
+BF16 = jnp.bfloat16
+LAT = 96
+LON = 160
+GROUP = 4
+HALF = 384
+ROWS = 208
+FCHUNK = 512
+VMEM_BYTES = 56 * 1024 * 1024
+SCHED = pltpu.CompilerParams(vmem_limit_bytes=VMEM_BYTES)
+
+
+def fits(parts):
+    return LAT % (parts * GROUP) == 0 and LON // 2 % (2 * parts) == 0
+
+
+def dot(left, right, left_dim, right_dim):
+    return lax.dot_general(
+        left, right, (((left_dim,), (right_dim,)), ((), ())), preferred_element_type=F32
+    )
+
+
+def gelu_pair(values):
+    cdf = 0.5 + 0.5 * lax.erf(values * math.sqrt(0.5))
+    pdf = jnp.exp2(values * values * (-0.5 * math.log2(math.e))) * (1.0 / math.sqrt(2.0 * math.pi))
+    return (values * cdf, cdf + values * pdf)
+
+
+@functools.lru_cache(maxsize=None)
+def lon_matrix():
+    slots = LON // 2
+    points = np.arange(LON)
+    table = np.zeros((slots, 2, LON))
+    for slot in range(slots):
+        angles = 2.0 * np.pi * (slot * points % LON) / LON
+        table[slot, 0] = np.cos(angles)
+        table[slot, 1] = -np.sin(angles)
+    table[0, 1] = np.where(points % 2 == 0, 1.0, -1.0)
+    table /= np.sqrt(LON)
+    full = np.zeros((slots, 2, GROUP, GROUP, LON))
+    for row in range(GROUP):
+        full[:, :, row, row, :] = table
+    return full.reshape(slots * 2 * GROUP, GROUP * LON)
+
+
+@functools.lru_cache(maxsize=None)
+def lat_matrices(parts):
+    per_part = LAT // parts
+    groups = per_part // GROUP
+    forward = np.zeros((2, 2, ROWS, LAT, 2, 2))
+    share = np.zeros((2, ROWS))
+    lat = np.arange(LAT)
+
+    def put_plain(variant, start, slot):
+        for mode in range(LAT):
+            angles = 2.0 * np.pi * (mode * lat % LAT) / LAT
+            forward[variant, 0, start + mode, :, slot, 0] = np.cos(angles)
+            forward[variant, 0, start + mode, :, slot, 1] = np.sin(angles)
+            forward[variant, 1, start + mode, :, slot, 0] = -np.sin(angles)
+            forward[variant, 1, start + mode, :, slot, 1] = np.cos(angles)
+            share[variant, start + mode] = 1.0
+
+    half = LAT // 2 + 1
+    for column in range(2):
+        for mode in range(half):
+            angles = 2.0 * np.pi * (mode * lat % LAT) / LAT
+            row = column * half + mode
+            own = mode in (0, LAT // 2)
+            forward[0, 0, row, :, 0, column] = np.cos(angles)
+            forward[0, 1, row, :, 0, column] = 0.0 if own else -np.sin(angles)
+            share[0, row] = 0.5 if own else 1.0
+    put_plain(0, 2 * half, 1)
+    put_plain(1, 0, 0)
+    put_plain(1, LAT, 1)
+    forward /= np.sqrt(LAT)
+    forward = forward.reshape(2, 2, ROWS, parts, groups, GROUP, 2, 2)
+    forward = forward.transpose(0, 1, 2, 3, 4, 6, 7, 5)
+    shift_row = np.zeros((2, ROWS, 128))
+    shift_row[0, 0] = np.sqrt(LAT * LON)
+    return (forward, share, shift_row)
+
+
+def lat_tables(parts):
+    forward, share, shift_row = lat_matrices(parts)
+    tall = 2 * ROWS
+    wide = forward[0].size // tall
+    by_part = forward.reshape(2, tall, wide)
+    by_group = forward.transpose(0, 1, 2, 4, 3, 5, 6, 7).reshape(2, tall, wide)
+    weights = np.concatenate([share, share], axis=1)[:, :, None]
+    tables = (
+        by_part,
+        (weights * by_group).transpose(0, 2, 1),
+        weights * by_group,
+        by_part.transpose(0, 2, 1),
+    )
+    return tuple(jnp.asarray(table, BF16) for table in tables) + (jnp.asarray(shift_row, F32),)
+
+
+def normalise(values):
+    center = values - jnp.mean(values, axis=-1, keepdims=True)
+    inv_std = lax.rsqrt(jnp.mean(center * center, axis=-1, keepdims=True) + NORM_EPS)
+    return (center * inv_std, inv_std)
+
+
+def spread_body(tokens_ref, table_ref, low_ref, high_ref):
+    values = tokens_ref[...].astype(F32).reshape(GROUP * LON, 2 * HALF)
+    normed, _ = normalise(values)
+    out = dot(table_ref[...], normed.astype(BF16), 1, 0).astype(BF16)
+    low_ref[...] = out[:, :HALF].reshape(low_ref.shape)
+    high_ref[...] = out[:, HALF:].reshape(high_ref.shape)
+
+
+def spread(tokens, table, parts):
+    groups = tokens.shape[1] // GROUP
+    pairs = LON // 4 // parts
+    shape = (parts, groups, pairs, 16, HALF)
+    block = pl.BlockSpec((parts, 1, pairs, 16, HALF), lambda r: (0, r, 0, 0, 0))
+    return pl.pallas_call(
+        spread_body,
+        name="norm_and_longitude",
+        grid=(groups,),
+        in_specs=[
+            pl.BlockSpec((1, GROUP, LON, 2 * HALF), lambda r: (0, r, 0, 0)),
+            pl.BlockSpec(table.shape, lambda r: (0, 0)),
+        ],
+        out_specs=[block, block],
+        out_shape=[jax.ShapeDtypeStruct(shape, BF16)] * 2,
+        compiler_params=SCHED,
+    )(tokens, table)
+
+
+def filter_body(
+    groups,
+    pick_ref,
+    arrived_ref,
+    forward_ref,
+    inverse_ref,
+    shift_row_ref,
+    params_ref,
+    one_ref,
+    two_ref,
+    *outs,
+):
+    back_refs = outs[:groups]
+    modes_ref, sums_ref, slopes_ref = outs[groups:]
+    columns = forward_ref.shape[-1]
+    arrived = arrived_ref[...].reshape(columns, HALF)
+    raw = dot(forward_ref[0], arrived, 1, 0)
+    gain = params_ref[0:1, :]
+    shift = params_ref[1:2, :]
+    modes_re = (raw[:ROWS] * gain + shift_row_ref[0, :, 0:1] * shift).astype(BF16)
+    modes_im = (raw[ROWS:] * gain).astype(BF16)
+    modes_ref[0, :ROWS] = modes_re
+    modes_ref[0, ROWS:] = modes_im
+    from_re = dot(modes_re, one_ref[0], 1, 0)
+    from_im = dot(modes_im, one_ref[0], 1, 0)
+    bias_re = params_ref[4:5, :]
+    bias_im = params_ref[5:6, :]
+    re_a = from_re[:, :HALF] + bias_re
+    re_b = from_re[:, HALF:] + bias_im
+    im_a = from_im[:, :HALF]
+    im_b = from_im[:, HALF:]
+    plus_re, slope = gelu_pair(re_a - im_b)
+    slopes_ref[0, 0] = slope.astype(BF16)
+    minus_re, slope = gelu_pair(re_a + im_b)
+    slopes_ref[0, 1] = slope.astype(BF16)
+    sums_ref[0, 0, :, :HALF] = (plus_re + minus_re).astype(BF16)
+    sums_ref[0, 1, :, HALF:] = (plus_re - minus_re).astype(BF16)
+    plus_im, slope = gelu_pair(re_b + im_a)
+    slopes_ref[0, 2] = slope.astype(BF16)
+    minus_im, slope = gelu_pair(re_b - im_a)
+    slopes_ref[0, 3] = slope.astype(BF16)
+    sums_ref[0, 0, :, HALF:] = (-plus_im - minus_im).astype(BF16)
+    sums_ref[0, 1, :, :HALF] = (plus_im - minus_im).astype(BF16)
+    two_bias_re = params_ref[6:7, :]
+    two_bias_im = params_ref[7:8, :]
+    two_re = dot(sums_ref[0, 0], two_ref[0], 1, 0) + (two_bias_re + two_bias_re)
+    two_im = dot(sums_ref[0, 1], two_ref[0], 1, 0) + (two_bias_im - two_bias_im)
+    both = jnp.concatenate([two_re.astype(BF16), two_im.astype(BF16)], axis=0)
+    back = dot(inverse_ref[0], both, 1, 0).astype(BF16)
+    step = columns // groups
+    for group in range(groups):
+        ref = back_refs[group]
+        ref[...] = back[group * step : (group + 1) * step].reshape(ref.shape)
+
+
+def filter_forward(pick, arrived, tables, params, one, two, part_of_channels):
+    parts, groups, pairs = arrived.shape[:3]
+    forward, inverse, _, _, shift_row = tables
+    q = part_of_channels
+    tall = 2 * ROWS
+
+    def chosen(*shape):
+        return pl.BlockSpec((1,) + shape, lambda b, pick_ref: (pick_ref[b], 0, 0))
+
+    def fixed(*shape):
+        return pl.BlockSpec((1,) + shape, lambda b, pick_ref: (q, 0, 0))
+
+    def stepped(*shape):
+        zeros = (0,) * len(shape)
+        return pl.BlockSpec((1,) + shape, lambda b, pick_ref: (b,) + zeros)
+
+    back_block = pl.BlockSpec((parts, 1, 16, HALF), lambda b, pick_ref: (0, b, 0, 0))
+    columns = forward.shape[-1]
+    return pl.pallas_call(
+        functools.partial(filter_body, groups),
+        name="filter_forward",
+        grid_spec=pltpu.PrefetchScalarGridSpec(
+            num_scalar_prefetch=1,
+            grid=(pairs,),
+            in_specs=[
+                pl.BlockSpec((parts, groups, 1, 16, HALF), lambda b, pick_ref: (0, 0, b, 0, 0)),
+                chosen(tall, columns),
+                chosen(columns, tall),
+                chosen(ROWS, 128),
+                pl.BlockSpec((16, HALF), lambda b, pick_ref: (0, q)),
+                fixed(HALF, 2 * HALF),
+                fixed(2 * HALF, HALF),
+            ],
+            out_specs=[back_block] * groups
+            + [stepped(tall, HALF), stepped(2, ROWS, 2 * HALF), stepped(4, ROWS, HALF)],
+        ),
+        out_shape=[jax.ShapeDtypeStruct((parts, pairs, 16, HALF), BF16)] * groups
+        + [
+            jax.ShapeDtypeStruct((pairs, tall, HALF), BF16),
+            jax.ShapeDtypeStruct((pairs, 2, ROWS, 2 * HALF), BF16),
+            jax.ShapeDtypeStruct((pairs, 4, ROWS, HALF), BF16),
+        ],
+        compiler_params=SCHED,
+    )(pick, arrived, forward, inverse, shift_row, params, one, two)
+
+
+def filter_back_body(
+    groups,
+    pick_ref,
+    *refs,
+):
+    arrived_refs = refs[:groups]
+    adjoint_ref, inverse_ref, one_ref, two_ref, modes_ref, sums_ref, slopes_ref = refs[
+        groups : groups + 7
+    ]
+    sent_ref, one_grad_ref, two_grad_ref, bias_ref = refs[groups + 7 :]
+    columns = adjoint_ref.shape[-1]
+    step = columns // groups
+    arrived = jnp.concatenate([ref[...].reshape(step, HALF) for ref in arrived_refs], axis=0)
+    grad = dot(adjoint_ref[0], arrived, 1, 0)
+    grad_re = grad[:ROWS].astype(BF16)
+    grad_im = grad[ROWS:].astype(BF16)
+    from_re = dot(grad_re, two_ref[0], 1, 1)
+    from_im = dot(grad_im, two_ref[0], 1, 1)
+    du = from_re[:, :HALF]
+    dv = -from_re[:, HALF:]
+    dw = from_im[:, :HALF]
+    dx = from_im[:, HALF:]
+    plus_re = (du + dx) * slopes_ref[0, 0].astype(F32)
+    minus_re = (du - dx) * slopes_ref[0, 1].astype(F32)
+    plus_im = (dv + dw) * slopes_ref[0, 2].astype(F32)
+    minus_im = (dv - dw) * slopes_ref[0, 3].astype(F32)
+    re_a = plus_re + minus_re
+    im_b = minus_re - plus_re
+    im_a = plus_im - minus_im
+    re_b = plus_im + minus_im
+    out_re = jnp.concatenate([re_a.astype(BF16), re_b.astype(BF16)], axis=1)
+    out_im = jnp.concatenate([im_a.astype(BF16), im_b.astype(BF16)], axis=1)
+    modes_re = dot(out_re, one_ref[0], 1, 1)
+    modes_im = dot(out_im, one_ref[0], 1, 1)
+    both = jnp.concatenate([modes_re.astype(BF16), modes_im.astype(BF16)], axis=0)
+    sent = dot(inverse_ref[0], both, 1, 0).astype(BF16)
+    sent_ref[...] = sent.reshape(sent_ref.shape)
+    one_part = dot(modes_ref[0, :ROWS], out_re, 0, 0) + dot(modes_ref[0, ROWS:], out_im, 0, 0)
+    two_part = dot(sums_ref[0, 0], grad_re, 0, 0) + dot(sums_ref[0, 1], grad_im, 0, 0)
+    rows = [jnp.sum(part, axis=0, keepdims=True) for part in (re_a, re_b, grad[:ROWS], grad[ROWS:])]
+    bias_part = jnp.concatenate(rows + [jnp.zeros((4, HALF), F32)], axis=0)
+    first = pl.program_id(0) == 0
+
+    @pl.when(first)
+    def _():
+        one_grad_ref[...] = one_part
+        two_grad_ref[...] = two_part
+        bias_ref[...] = bias_part
+
+    @pl.when(jnp.logical_not(first))
+    def _():
+        one_grad_ref[...] += one_part
+        two_grad_ref[...] += two_part
+        bias_ref[...] += bias_part
+
+
+def filter_backward(pick, arrived, tables, one, two, modes, sums, slopes, part_of_channels):
+    groups = len(arrived)
+    parts, pairs = arrived[0].shape[:2]
+    _, _, adjoint, inverse, _ = tables
+    q = part_of_channels
+    tall = 2 * ROWS
+    columns = adjoint.shape[-1]
+
+    def chosen(*shape):
+        return pl.BlockSpec((1,) + shape, lambda b, pick_ref: (pick_ref[b], 0, 0))
+
+    def fixed(*shape):
+        return pl.BlockSpec((1,) + shape, lambda b, pick_ref: (q, 0, 0))
+
+    def stepped(*shape):
+        zeros = (0,) * len(shape)
+        return pl.BlockSpec((1,) + shape, lambda b, pick_ref: (b,) + zeros)
+
+    def whole(*shape):
+        return pl.BlockSpec(shape, lambda b, pick_ref: (0,) * len(shape))
+
+    arrived_block = pl.BlockSpec((parts, 1, 16, HALF), lambda b, pick_ref: (0, b, 0, 0))
+    return pl.pallas_call(
+        functools.partial(filter_back_body, groups),
+        name="filter_backward",
+        grid_spec=pltpu.PrefetchScalarGridSpec(
+            num_scalar_prefetch=1,
+            grid=(pairs,),
+            in_specs=[arrived_block] * groups
+            + [
+                chosen(tall, columns),
+                chosen(columns, tall),
+                fixed(HALF, 2 * HALF),
+                fixed(2 * HALF, HALF),
+                stepped(tall, HALF),
+                stepped(2, ROWS, 2 * HALF),
+                stepped(4, ROWS, HALF),
+            ],
+            out_specs=[
+                pl.BlockSpec((parts, groups, 1, 16, HALF), lambda b, pick_ref: (0, 0, b, 0, 0)),
+                whole(HALF, 2 * HALF),
+                whole(2 * HALF, HALF),
+                whole(8, HALF),
+            ],
+        ),
+        out_shape=[
+            jax.ShapeDtypeStruct((parts, groups, pairs, 16, HALF), BF16),
+            jax.ShapeDtypeStruct((HALF, 2 * HALF), F32),
+            jax.ShapeDtypeStruct((2 * HALF, HALF), F32),
+            jax.ShapeDtypeStruct((8, HALF), F32),
+        ],
+        compiler_params=SCHED,
+    )(pick, *arrived, adjoint, inverse, one, two, modes, sums, slopes)
+
+
+def dense_body(
+    tokens_ref,
+    cotangent_ref,
+    low_ref,
+    high_ref,
+    inverse_ref,
+    table_ref,
+    params_ref,
+    in_bias_ref,
+    in_ref,
+    out_ref,
+    result_ref,
+    mixed_grad_ref,
+    low_sent_ref,
+    high_sent_ref,
+    second_ref,
+    grad_low_ref,
+    act_ref,
+    grad_pre_ref,
+    in_bias_grad_ref,
+    rows_ref,
+    mixed_ref,
+    branch_ref,
+    grad_second_ref,
+):
+    chunk = pl.program_id(0)
+    count = GROUP * LON
+    wide = 2 * HALF
+
+    @pl.when(chunk == 0)
+    def _():
+        inputs = tokens_ref[...].astype(F32).reshape(count, wide)
+        normed, _ = normalise(inputs)
+        base = normed * params_ref[0:1, :] + params_ref[1:2, :] + inputs
+        mixed_ref[:, :HALF] = (
+            dot(inverse_ref[...], low_ref[...].reshape(count, HALF), 1, 0) + base[:, :HALF]
+        )
+        mixed_ref[:, HALF:] = (
+            dot(inverse_ref[...], high_ref[...].reshape(count, HALF), 1, 0) + base[:, HALF:]
+        )
+        normed_two, _ = normalise(mixed_ref[...])
+        second_ref[...] = (normed_two * params_ref[2:3, :] + params_ref[3:4, :]).astype(BF16)
+        grad_low_ref[...] = (
+            cotangent_ref[...].astype(F32).reshape(count, wide) * params_ref[13:14, :]
+        ).astype(BF16)
+        branch_ref[...] = jnp.zeros_like(branch_ref)
+        grad_second_ref[...] = jnp.zeros_like(grad_second_ref)
+
+    pre = dot(second_ref[...], in_ref[...], 1, 0) + in_bias_ref[...]
+    grad_act = dot(grad_low_ref[...], out_ref[...], 1, 1)
+    act, slope = gelu_pair(pre)
+    act = act.astype(BF16)
+    grad_pre = grad_act * slope
+    in_bias_grad_ref[...] = jnp.sum(grad_pre, axis=0, keepdims=True)
+    grad_pre = grad_pre.astype(BF16)
+    act_ref[...] = act
+    grad_pre_ref[...] = grad_pre
+    branch_ref[...] += dot(act, out_ref[...], 1, 0)
+    grad_second_ref[...] += dot(grad_pre, in_ref[...], 1, 1)
+
+    @pl.when(chunk == pl.num_programs(0) - 1)
+    def _():
+        mixed = mixed_ref[...]
+        result = (mixed + branch_ref[...] + params_ref[8:9, :]).astype(BF16)
+        result_ref[...] = result.reshape(result_ref.shape)
+        normed_two, inv_two = normalise(mixed)
+        upstream = grad_second_ref[...]
+        scaled = upstream * params_ref[2:3, :]
+        first_mean = jnp.mean(scaled, axis=-1, keepdims=True)
+        second_mean = jnp.mean(scaled * normed_two, axis=-1, keepdims=True)
+        grad_out = cotangent_ref[...].astype(F32).reshape(count, wide) * params_ref[13:14, :]
+        mixed_grad = grad_out + inv_two * (scaled - first_mean - normed_two * second_mean)
+        mixed_grad_ref[...] = mixed_grad.reshape(mixed_grad_ref.shape)
+        rows = [
+            jnp.sum(part, axis=0, keepdims=True)
+            for part in (upstream * normed_two, upstream, grad_low_ref[...].astype(F32))
+        ]
+        rows_ref[...] = jnp.concatenate(rows + [jnp.zeros((5, wide), F32)], axis=0)
+        sent = dot(table_ref[...], mixed_grad.astype(BF16), 1, 0).astype(BF16)
+        low_sent_ref[...] = sent[:, :HALF].reshape(low_sent_ref.shape)
+        high_sent_ref[...] = sent[:, HALF:].reshape(high_sent_ref.shape)
+
+
+def dense(tokens, cotangent, low, high, inverse, table, params, in_bias, in_work, out_work, group):
+    parts, pairs = low.shape[:2]
+    count = GROUP * LON
+    wide = 2 * HALF
+    hidden = in_work.shape[1]
+
+    def whole(*shape):
+        return pl.BlockSpec(shape, lambda f: (0,) * len(shape))
+
+    rows_in = pl.BlockSpec((1, GROUP, LON, wide), lambda f: (0, group, 0, 0))
+    sent = whole(parts, pairs, 16, HALF)
+    return pl.pallas_call(
+        dense_body,
+        name="dense_group",
+        grid=(hidden // FCHUNK,),
+        in_specs=[
+            rows_in,
+            rows_in,
+            sent,
+            sent,
+            whole(*inverse.shape),
+            whole(*table.shape),
+            whole(16, wide),
+            pl.BlockSpec((1, FCHUNK), lambda f: (0, f)),
+            pl.BlockSpec((wide, FCHUNK), lambda f: (0, f)),
+            pl.BlockSpec((FCHUNK, wide), lambda f: (f, 0)),
+        ],
+        out_specs=[
+            whole(GROUP, LON, wide),
+            whole(GROUP, LON, wide),
+            sent,
+            sent,
+            whole(count, wide),
+            whole(count, wide),
+            pl.BlockSpec((count, FCHUNK), lambda f: (0, f)),
+            pl.BlockSpec((count, FCHUNK), lambda f: (0, f)),
+            pl.BlockSpec((1, FCHUNK), lambda f: (0, f)),
+            whole(8, wide),
+        ],
+        out_shape=[
+            jax.ShapeDtypeStruct((GROUP, LON, wide), BF16),
+            jax.ShapeDtypeStruct((GROUP, LON, wide), F32),
+            jax.ShapeDtypeStruct((parts, pairs, 16, HALF), BF16),
+            jax.ShapeDtypeStruct((parts, pairs, 16, HALF), BF16),
+            jax.ShapeDtypeStruct((count, wide), BF16),
+            jax.ShapeDtypeStruct((count, wide), BF16),
+            jax.ShapeDtypeStruct((count, hidden), BF16),
+            jax.ShapeDtypeStruct((count, hidden), BF16),
+            jax.ShapeDtypeStruct((1, hidden), F32),
+            jax.ShapeDtypeStruct((8, wide), F32),
+        ],
+        scratch_shapes=[pltpu.VMEM((count, wide), F32)] * 3,
+        compiler_params=SCHED,
+    )(tokens, cotangent, low, high, inverse, table, params, in_bias, in_work, out_work)
+
+
+def gather_grad_body(groups, *refs):
+    tokens_ref = refs[0]
+    mixed_grad_refs = refs[1 : 1 + groups]
+    low_ref, high_ref, inverse_ref, params_ref, grad_ref, rows_ref = refs[1 + groups :]
+    step = pl.program_id(0)
+    count = GROUP * LON
+    wide = 2 * HALF
+    mixed_grad = mixed_grad_refs[0][...]
+    for group in range(1, groups):
+        mixed_grad = jnp.where(step == group, mixed_grad_refs[group][...], mixed_grad)
+    mixed_grad = mixed_grad.reshape(count, wide)
+    low = dot(inverse_ref[...], low_ref[...].reshape(count, HALF), 1, 0)
+    high = dot(inverse_ref[...], high_ref[...].reshape(count, HALF), 1, 0)
+    upstream = mixed_grad + jnp.concatenate([low, high], axis=1)
+    normed, inv_std = normalise(tokens_ref[...].astype(F32).reshape(count, wide))
+    scaled = upstream * params_ref[0:1, :]
+    first_mean = jnp.mean(scaled, axis=-1, keepdims=True)
+    second_mean = jnp.mean(scaled * normed, axis=-1, keepdims=True)
+    out = mixed_grad + inv_std * (scaled - first_mean - normed * second_mean)
+    grad_ref[...] = out.reshape(grad_ref.shape)
+    rows = [jnp.sum(part, axis=0, keepdims=True) for part in (upstream * normed, upstream)]
+    part = jnp.concatenate(rows + [jnp.zeros((6, wide), F32)], axis=0)
+
+    @pl.when(step == 0)
+    def _():
+        rows_ref[...] = part
+
+    @pl.when(step > 0)
+    def _():
+        rows_ref[...] += part
+
+
+def gather_grad(tokens, mixed_grads, low, high, inverse, params):
+    parts, groups, pairs = low.shape[:3]
+    wide = 2 * HALF
+
+    def whole(*shape):
+        return pl.BlockSpec(shape, lambda r: (0,) * len(shape))
+
+    rows = pl.BlockSpec((1, GROUP, LON, wide), lambda r: (0, r, 0, 0))
+    arrived = pl.BlockSpec((parts, 1, pairs, 16, HALF), lambda r: (0, r, 0, 0, 0))
+    return pl.pallas_call(
+        functools.partial(gather_grad_body, groups),
+        name="longitude_and_norm_grad",
+        grid=(groups,),
+        in_specs=[rows]
+        + [whole(GROUP, LON, wide)] * groups
+        + [arrived, arrived, whole(*inverse.shape), whole(16, wide)],
+        out_specs=[rows, whole(8, wide)],
+        out_shape=[
+            jax.ShapeDtypeStruct((1, groups * GROUP, LON, wide), F32),
+            jax.ShapeDtypeStruct((8, wide), F32),
+        ],
+        compiler_params=SCHED,
+    )(tokens, *mixed_grads, low, high, inverse, params)
+
+
+def block_matrices(weight):
+    size = weight.shape[1] // 2
+    count = HALF // size
+    grouped = weight.reshape(2, count, size, 2, size)
+    eye = jnp.eye(count, dtype=weight.dtype)
+    full = grouped[:, :, :, :, None, :] * eye[None, :, None, None, :, None]
+    return full.reshape(2, HALF, 2, HALF)
+
+
+def own_blocks(matrix, size):
+    count = HALF // size
+    return jnp.concatenate(
+        [matrix[i * size : (i + 1) * size, i * size : (i + 1) * size] for i in range(count)], axis=0
+    )
+
+
+def exchange(values):
+    return lax.all_to_all(values, "sp", split_axis=0, concat_axis=0, tiled=True)
+
+
+def fast_shards(
+    sizes,
+    tokens,
+    cotangent,
+    storm_weight,
+    filter_master,
+    in_master,
+    out_master,
+    small_master,
+    filter_m,
+    filter_v,
+    in_m,
+    in_v,
+    out_m,
+    out_v,
+    small_m,
+    small_v,
+    filter_ema,
+    in_ema,
+    out_ema,
+    small_ema,
+):
+    both = ("samp", "sp")
+    parts = sizes[1]
+    devices = sizes[0] * sizes[1]
+    groups = tokens.shape[1] // GROUP
+    pairs = LON // 4 // parts
+    width = tokens.shape[-1]
+    block = width // NB
+    small_share = small_master.shape[0]
+    sp_index = lax.axis_index("sp")
+
+    lon = lon_matrix()
+    lon_table = jnp.asarray(lon, BF16)
+    lon_back = jnp.asarray(lon.T, BF16)
+    tables = lat_tables(parts)
+    pick = jnp.where((sp_index == 0) & (jnp.arange(pairs) == 0), 0, 1).astype(jnp.int32)
+
+    filter_rows = filter_master.shape[0]
+    small_line = jnp.pad(small_master.astype(BF16), (0, 4 * block - small_share)).reshape(1, -1)
+    packed = jnp.concatenate([filter_master.astype(BF16), small_line], axis=0)
+    sent = spread(tokens, lon_table, parts)
+    packed_all = lax.all_gather(packed, both, axis=0, tiled=True).reshape(devices, filter_rows + 1, -1)
+    filter_work = packed_all[:, :filter_rows].reshape(width, 4 * block)
+    small_work = packed_all[:, filter_rows, :small_share].reshape(-1)
+    in_work = lax.all_gather(in_master.astype(BF16), both, axis=0, tiled=True)
+    out_work = lax.all_gather(out_master.astype(BF16), both, axis=0, tiled=True)
+
+    params = small_work.astype(F32).reshape(13, width)
+    scale = storm_weight.astype(F32)[0] / 64.0
+    in_bias = params[9:13].reshape(1, -1)
+    params = jnp.concatenate(
+        [params, jnp.full((1, width), scale, F32), jnp.zeros((2, width), F32)], axis=0
+    )
+    one = block_matrices(filter_work[:, : 2 * block]).reshape(2, HALF, 2 * HALF)
+    two = block_matrices(filter_work[:, 2 * block :]).transpose(0, 2, 1, 3).reshape(2, 2 * HALF, HALF)
+
+    arrived = [exchange(piece) for piece in sent]
+    forward = [
+        filter_forward(pick, arrived[q], tables, params, one, two, q) for q in range(2)
+    ]
+    returned = [[exchange(forward[q][group]) for q in range(2)] for group in range(groups)]
+    dense_out = [
+        dense(
+            tokens,
+            cotangent,
+            returned[group][0],
+            returned[group][1],
+            lon_back,
+            lon_table,
+            params,
+            in_bias,
+            in_work,
+            out_work,
+            group,
+        )
+        for group in range(groups)
+    ]
+    grad_arrived = [[exchange(dense_out[group][2 + q]) for group in range(groups)] for q in range(2)]
+    backward = [
+        filter_backward(pick, grad_arrived[q], tables, one, two, *forward[q][groups:], q)
+        for q in range(2)
+    ]
+    grad_returned = [exchange(backward[q][0]) for q in range(2)]
+    input_grad, norm_rows = gather_grad(
+        tokens, [part[1] for part in dense_out], grad_returned[0], grad_returned[1], lon_back, params
+    )
+    result = jnp.concatenate([part[0] for part in dense_out], axis=0)[None]
+
+    second, grad_low, act, grad_pre = (
+        jnp.concatenate([part[i] for part in dense_out], axis=0) for i in (4, 5, 6, 7)
+    )
+    out_local = jnp.einsum("tf,td->fd", act, grad_low, preferred_element_type=F32).astype(BF16)
+    in_local = jnp.einsum("td,tf->df", second, grad_pre, preferred_element_type=F32).astype(BF16)
+    in_grad = lax.psum_scatter(in_local, both, scatter_dimension=0, tiled=True).astype(F32)
+    out_grad = lax.psum_scatter(out_local, both, scatter_dimension=0, tiled=True).astype(F32)
+
+    pieces = []
+    for q in range(2):
+        one_grad = backward[q][1]
+        two_grad = backward[q][2]
+        pieces.append(
+            jnp.concatenate(
+                [
+                    own_blocks(one_grad[:, :HALF], block),
+                    own_blocks(one_grad[:, HALF:], block),
+                    own_blocks(two_grad[:HALF], block),
+                    own_blocks(two_grad[HALF:], block),
+                ],
+                axis=1,
+            )
+        )
+    filter_local = jnp.concatenate(pieces, axis=0)
+    filter_grad = lax.psum_scatter(filter_local, both, scatter_dimension=0, tiled=True)
+
+    bias_rows = jnp.concatenate([backward[0][3], backward[1][3]], axis=1)
+    dense_rows = sum(part[9] for part in dense_out)
+    in_bias_grad = sum(part[8] for part in dense_out)
+    small_local = jnp.concatenate(
+        [
+            norm_rows[0:2],
+            dense_rows[0:2],
+            bias_rows[0:2],
+            bias_rows[2:3] + bias_rows[2:3],
+            bias_rows[3:4] - bias_rows[3:4],
+            dense_rows[2:3],
+            in_bias_grad.reshape(4, width),
+        ],
+        axis=0,
+    ).reshape(-1)
+    small_grad = lax.psum_scatter(small_local, both, scatter_dimension=0, tiled=True)
+
+    filter_new, filter_m_new, filter_v_new, filter_ema_new = adam_update(
+        filter_master, filter_grad, filter_m, filter_v, filter_ema, 0.2
+    )
+    in_new, in_m_new, in_v_new, in_ema_new = adam_update(
+        in_master, in_grad, in_m, in_v, in_ema, 0.1
+    )
+    out_new, out_m_new, out_v_new, out_ema_new = adam_update(
+        out_master, out_grad, out_m, out_v, out_ema, 0.05
+    )
+    small_new, small_m_new, small_v_new, small_ema_new = adam_update(
+        small_master, small_grad, small_m, small_v, small_ema, 0.5
+    )
+    return (
+        result,
+        input_grad,
+        filter_grad,
+        in_grad,
+        out_grad,
+        small_grad,
+        filter_new,
+        in_new,
+        out_new,
+        small_new,
+        filter_m_new,
+        filter_v_new,
+        in_m_new,
+        in_v_new,
+        out_m_new,
+        out_v_new,
+        small_m_new,
+        small_v_new,
+        filter_ema_new,
+        in_ema_new,
+        out_ema_new,
+        small_ema_new,
+    )
+
+
 def solution(mesh):
+    sizes = (mesh.shape["samp"], mesh.shape["sp"])
+    body = functools.partial(fast_shards, sizes) if fits(sizes[1]) else plain_shards
     return jax.shard_map(
-        shards,
+        body,
         mesh=mesh,
         in_specs=(
             P("samp", "sp", None, None),

time: 1710 us -> 840 us (0.49)
  local copies, waits for them, and re-layouts: 336 us -> 19.5 us
  matrix products: 311 us -> 29.2 us
  other arithmetic: 203 us -> 23.5 us
  waiting for transfers between devices: 413 us -> 237 us
  Pallas kernels: 0 us -> 157 us
  blocking collectives: 404 us -> 311 us
  starting transfers between devices: 15.2 us -> 37.8 us
    dot_general x24 -> x2, matrix products: 311 us -> 29.2 us  [the longest x1 14.7 us: fast_shards(): jnp.einsum('tf,td->fd', act, grad_low, preferred_element_type=F32)]
    pallas_call x0 -> x9, Pallas kernels: none -> 157 us  [the longest x3 74.8 us: dense(): pl.pallas_call(dense_body, name='dense_group', grid=(hidden // FCHUNK,),...]
    all_to_all x3 -> x8, waiting for transfers between devices: 131 us -> 46 us  [exchange(): return lax.all_to_all(values, 'sp', split_axis=0, concat_axis=0, tiled=True)]
    convert_element_type x4 -> x2, local copies, waits for them, and re-layouts: 79.1 us -> 0.22 us  [fast_shards(): params = small_work.astype(F32).reshape(13, width)]
    all_gather x1, blocking collectives: 187 us -> 109 us  [fast_shards(): lax.all_gather(packed, both, axis=0, tiled=True)]
    all_gather x2, waiting for transfers between devices: 72.2 us -> 0.01 us  [the longest x1 0.01 us: fast_shards(): in_work = lax.all_gather(in_master.astype(BF16), both, axis=0, tiled=True)]
    another operation x13 -> x0, local copies, waits for them, and re-layouts: 70.6 us -> none
    sub x6 -> x0, local copies, waits for them, and re-layouts: 63.1 us -> none  [the longest x3 34.9 us: mix_back(): grad_imag = toward[:, :, 1, 0] - toward[:, :, 0, 1]]
  transfers between devices with their start and end apart: 8 -> 13, of which waited for: 5 -> 5; matrix products, arithmetic and copies ran while one was open for 16% -> 7% of each run, Pallas kernels for 0% -> 17%
where the time goes in v1:
time: 840 us; the launch traced here: 830 us
  blocking collectives  311 us (37%)
  waiting for transfers between devices  237 us (28%)
  Pallas kernels  157 us (19%)
  starting transfers between devices  37.8 us (4%)
  matrix products  29.2 us (3%)
  other arithmetic  23.5 us (3%)
  local copies, waits for them, and re-layouts  19.5 us (2%)
  between operations  15.4 us (2%)
    all_to_all x8, blocking collectives, exchange(): return lax.all_to_all(values, 'sp', split_axis=0, concat_axis=0, tiled=True)  165 us
    reduce_scatter x1, waiting for transfers between devices, fast_shards(): lax.psum_scatter(in_local, both, scatter_dimension=0, tiled=True)  110 us
    all_gather x1, blocking collectives, fast_shards(): lax.all_gather(packed, both, axis=0, tiled=True)  109 us
    pallas_call x3, Pallas kernels, dense(): pl.pallas_call(dense_body, name='dense_group', grid=(hidden // FCHUNK,),...  74.8 us
    reduce_scatter x1, waiting for transfers between devices, fast_shards(): lax.psum_scatter(out_local, both, scatter_dimension=0, tiled=True)  53.7 us
    all_to_all x8, waiting for transfers between devices, exchange(): return lax.all_to_all(values, 'sp', split_axis=0, concat_axis=0, tiled=True)  46 us
    unnamed x1, blocking collectives  37.3 us
    all_to_all x8, starting transfers between devices, exchange(): return lax.all_to_all(values, 'sp', split_axis=0, concat_axis=0, tiled=True)  36.9 us
  transfers between devices with their start and end apart: 13, of which 5 were waited for; matrix products, arithmetic and copies ran while one was open for 7% of the time, Pallas kernels for 17%

profile of v1, /device:TPU:0, one launch (start us, length us, event | category | flops | bytes accessed | tf_op | source)
XLA Modules:
  0.0 830.3 jit_solution(17610888981395469159)
XLA Ops:
  8.9 6.8 norm_and_longitude.1
  15.7 7.4 all-to-all-start.2
  23.8 43.2 %all-to-all-done.2.arrived_ref = bf16[8,3,5,16,384]{4,3,2,1,0:T(8,128)(2,1)S(1)} async-done(((bf16[8,3,5,16,384]{4,3,2,1,0:T(8,128)(2,1)}), bf16[8,3,5,16,384]{4,3,2,1,0:T(8,128)(2,1)S(1)}, u32[]{:S(2)}, u32[]{:S(2)}) %all-to-all-start.2) | async-done | bytes 1474592 | tf_op jit(solution)/shard_map/all_to_all | solution.py:848
  68.1 4.3 all-to-all-start
  72.4 109.4 %all-gather = bf16[32,25,384]{2,1,0:T(8,128)(2,1)S(1)} all-gather(bf16[1,25,384]{2,1,0:T(8,128)(2,1)S(1)} %maximum_bitcast_fusion.1), channel_id=1, replica_groups=mesh['samp'=4,'sp'=8] {'samp','sp'}, dimensions={0}, use_global_device_ids=true | all-gather | bytes 633600 | tf_op jit(solution)/shard_map/all_gather | solution.py:893
  196.3 13.7 %filter_forward.3 = (bf16[8,5,16,384]{3,2,1,0:T(8,128)(2,1)}, bf16[8,5,16,384]{3,2,1,0:T(8,128)(2,1)}, bf16[8,5,16,384]{3,2,1,0:T(8,128)(2,1)}, bf16[5,416,384]{...) custom-call(s32[5]{0:T(128)} %and_select_fusion.pick_ref, ...), custom_call_target="tpu_custom_call" | custom-call | tf_op jit(solution)/shard_map/filter_forward/pallas_call | solution.py:496
  213.5 13.8 %filter_forward.2 = (bf16[8,5,16,384]{3,2,1,0:T(8,128)(2,1)}, bf16[8,5,16,384]{3,2,1,0:T(8,128)(2,1)}, bf16[8,5,16,384]{3,2,1,0:T(8,128)(2,1)}, bf16[5,416,384]{...) custom-call(s32[5]{0:T(128)} %and_select_fusion.pick_ref, ...), custom_call_target="tpu_custom_call" | custom-call | tf_op jit(solution)/shard_map/filter_forward/pallas_call | solution.py:496
  227.3 17.6 %all_to_all.80.low_ref = bf16[8,5,16,384]{3,2,1,0:T(8,128)(2,1)} all-to-all(bf16[8,5,16,384]{3,2,1,0:T(8,128)(2,1)} %get-tuple-element.77), channel_id=1, replica_groups=mesh['samp'=4,'sp'=8] {'sp'}, dimensions={0} | all-to-all | bytes 983040 | tf_op jit(solution)/shard_map/all_to_all | solution.py:848
  245.0 16.3 %all_to_all.81.high_ref = bf16[8,5,16,384]{3,2,1,0:T(8,128)(2,1)} all-to-all(bf16[8,5,16,384]{3,2,1,0:T(8,128)(2,1)S(1)} %copy-done.18), channel_id=1, replica_groups=mesh['samp'=4,'sp'=8] {'sp'}, dimensions={0} | all-to-all | bytes 983040 | tf_op jit(solution)/shard_map/all_to_all | solution.py:848
  261.2 16.9 %all_to_all.82.low_ref = bf16[8,5,16,384]{3,2,1,0:T(8,128)(2,1)} all-to-all(bf16[8,5,16,384]{3,2,1,0:T(8,128)(2,1)S(1)} %copy-done.19), channel_id=1, replica_groups=mesh['samp'=4,'sp'=8] {'sp'}, dimensions={0} | all-to-all | bytes 983040 | tf_op jit(solution)/shard_map/all_to_all | solution.py:848
  278.1 16.8 %all_to_all.83.high_ref = bf16[8,5,16,384]{3,2,1,0:T(8,128)(2,1)} all-to-all(bf16[8,5,16,384]{3,2,1,0:T(8,128)(2,1)S(1)} %copy-done.17), channel_id=1, replica_groups=mesh['samp'=4,'sp'=8] {'sp'}, dimensions={0} | all-to-all | bytes 983040 | tf_op jit(solution)/shard_map/all_to_all | solution.py:848
  294.9 4.2 all-to-all-start.6
  299.9 24.9 %dense_group.3 = (bf16[4,160,768]{2,1,0:T(8,128)(2,1)}, f32[4,160,768]{2,1,0:T(8,128)}, bf16[8,5,16,384]{3,2,1,0:T(8,128)(2,1)}, bf16[8,5,16,384]{3,2,1,0:T(8,12...) custom-call(bf16[1,12,160,768]{3,2,1,0:T(8,128)(2,1)} %refs_0_.1, ...), custom_call_target="tpu_custom_call" | custom-call | tf_op jit(solution)/shard_map/dense_group/pallas_call | solution.py:729
  324.8 6.2 all-to-all-start.12
  331.0 25.0 %dense_group.4 = (bf16[4,160,768]{2,1,0:T(8,128)(2,1)}, f32[4,160,768]{2,1,0:T(8,128)}, bf16[8,5,16,384]{3,2,1,0:T(8,128)(2,1)}, bf16[8,5,16,384]{3,2,1,0:T(8,12...) custom-call(bf16[1,12,160,768]{3,2,1,0:T(8,128)(2,1)} %refs_0_.1, ...), custom_call_target="tpu_custom_call" | custom-call | tf_op jit(solution)/shard_map/dense_group/pallas_call | solution.py:729
  356.1 18.3 %all_to_all.84.refs_1_ = bf16[8,5,16,384]{3,2,1,0:T(8,128)(2,1)} all-to-all(bf16[8,5,16,384]{3,2,1,0:T(8,128)(2,1)} %get-tuple-element.98), channel_id=1, replica_groups=mesh['samp'=4,'sp'=8] {'sp'}, dimensions={0} | all-to-all | bytes 983040 | tf_op jit(solution)/shard_map/all_to_all | solution.py:848
  374.4 16.2 %all_to_all.85.refs_0_ = bf16[8,5,16,384]{3,2,1,0:T(8,128)(2,1)} all-to-all(bf16[8,5,16,384]{3,2,1,0:T(8,128)(2,1)S(1)} %copy-done.16), channel_id=1, replica_groups=mesh['samp'=4,'sp'=8] {'sp'}, dimensions={0} | all-to-all | bytes 983040 | tf_op jit(solution)/shard_map/all_to_all | solution.py:848
  390.6 3.9 all-to-all-start.9
  394.5 24.9 %dense_group.5 = (bf16[4,160,768]{2,1,0:T(8,128)(2,1)}, f32[4,160,768]{2,1,0:T(8,128)}, bf16[8,5,16,384]{3,2,1,0:T(8,128)(2,1)}, bf16[8,5,16,384]{3,2,1,0:T(8,12...) custom-call(bf16[1,12,160,768]{3,2,1,0:T(8,128)(2,1)} %refs_0_.1, ...), custom_call_target="tpu_custom_call" | custom-call | tf_op jit(solution)/shard_map/dense_group/pallas_call | solution.py:729
  419.5 18.8 %all_to_all.86.refs_2_ = bf16[8,5,16,384]{3,2,1,0:T(8,128)(2,1)} all-to-all(bf16[8,5,16,384]{3,2,1,0:T(8,128)(2,1)} %get-tuple-element.92), channel_id=1, replica_groups=mesh['samp'=4,'sp'=8] {'sp'}, dimensions={0} | all-to-all | bytes 983040 | tf_op jit(solution)/shard_map/all_to_all | solution.py:848
  442.2 18.1 %filter_backward.2 = (bf16[8,3,5,16,384]{4,3,2,1,0:T(8,128)(2,1)}, f32[384,768]{1,0:T(8,128)}, f32[768,384]{1,0:T(8,128)}, f32[8,384]{1,0:T(8,128)}) custom-call(s32[5]{0:T(128)} %and_select_fusion.pick_ref, bf16[8,5,16,384]{3,2,1,0:T(8,128)(2,1)} %all_to_all.85.refs_0_, bf16[8,5,16,384]{3,2,1,0:T(8,128)(2,1)} %copy-done.8, ...), custom_call_target="tpu_custom_call" | custom-call | tf_op jit(solution)/shard_map/filter_backward/pallas_call | solution.py:602
  462.7 18.1 %filter_backward.3 = (bf16[8,3,5,16,384]{4,3,2,1,0:T(8,128)(2,1)}, f32[384,768]{1,0:T(8,128)}, f32[768,384]{1,0:T(8,128)}, f32[8,384]{1,0:T(8,128)}) custom-call(s32[5]{0:T(128)} %and_select_fusion.pick_ref, bf16[8,5,16,384]{3,2,1,0:T(8,128)(2,1)} %copy-done.4, bf16[8,5,16,384]{3,2,1,0:T(8,128)(2,1)} %all_to_all.84.refs_1_, ...), custom_call_target="tpu_custom_call" | custom-call | tf_op jit(solution)/shard_map/filter_backward/pallas_call | solution.py:602
  482.4 5.7 maximum_maximum_fusion
  488.6 14.7 %fusion.12 = bf16[3072,768]{1,0:T(8,128)(2,1)} fusion(bf16[640,3072]{1,0:T(8,128)(2,1)} %get-tuple-element.117, bf16[640,3072]{1,0:T(8,128)(2,1)} %get-tuple-element.116, bf16[640,3072]{1,0:T(8,128)(2,1)} %get-tuple-element.115, bf16[640,768]{1,0:T(8,128)(2,1)} %get-tuple-element.120, bf16[640,768]{1,0:T(8,128)(2,1)S(1)} %copy-done.44, ...), kind=kOutput, calls=%fused_computation.12 | convolution fusion | flops 9106292736 | bytes 19464192 | tf_op jit(solution)/shard_map/tf,td->fd/dot_general | solution.py:943
  505.2 14.4 %fusion.15 = bf16[768,3072]{1,0:T(8,128)(2,1)} fusion(bf16[640,3072]{1,0:T(8,128)(2,1)} %get-tuple-element.114, bf16[640,3072]{1,0:T(8,128)(2,1)} %get-tuple-element.113, bf16[640,3072]{1,0:T(8,128)(2,1)} %get-tuple-element.112, bf16[640,768]{1,0:T(8,128)(2,1)S(1)} %copy-done.45, bf16[640,768]{1,0:T(8,128)(2,1)S(1)} %copy-done.43, ...), kind=kOutput, calls=%fused_computation.13 | convolution fusion | flops 9106292736 | bytes 19464192 | tf_op jit(solution)/shard_map/td,tf->df/dot_general | solution.py:944
  521.0 43.8 %all_to_all.87.refs_5_ = bf16[8,3,5,16,384]{4,3,2,1,0:T(8,128)(2,1)} all-to-all(bf16[8,3,5,16,384]{4,3,2,1,0:T(8,128)(2,1)S(1)} %copy-done.10), channel_id=1, replica_groups=mesh['samp'=4,'sp'=8] {'sp'}, dimensions={0} | all-to-all | bytes 2949120 | tf_op jit(solution)/shard_map/all_to_all | solution.py:848
  564.8 3.9 all-to-all-start.11
  572.9 26.7 %reduce-scatter.10.cloned.1.call-done = f32[24,384]{1,0:T(8,128)} async-done(((f32[768,384]{1,0:T(8,128)}), f32[24,384]{1,0:T(8,128)}) %reduce-scatter.10.cloned.1.call-update) | async-done | bytes 36880
  605.1 11.6 %longitude_and_norm_grad.1 = (f32[1,12,160,768]{3,2,1,0:T(8,128)}, f32[8,768]{1,0:T(8,128)}) custom-call(bf16[1,12,160,768]{3,2,1,0:T(8,128)(2,1)} %refs_0_.1, f32[4,160,768]{2,1,0:T(8,128)} %get-tuple-element.87.refs_1_, f32[4,160,768]{2,1,0:T(8,128)} %get-tuple-element.88.refs_2_, f32[4,160,768]{2,1,0:T(8,128)} %get-tuple-element.89.refs_3_, ...), custom_call_target="tpu_custom_call" | custom-call | tf_op jit(solution)/shard_map/longitude_and_norm_grad/pallas_call | solution.py:815
  617.5 37.3 %all-reduce.2 = f32[9984]{0:T(1024)S(1)} all-reduce(f32[9984]{0:T(1024)S(1)} %reshape.99), channel_id=5, replica_groups=mesh['samp'=4,'sp'=8] {'samp','sp'}, use_global_device_ids=true, to_apply=%region_3.4.clone | all-reduce | flops 9984 | bytes 79872
  655.5 53.7 %reduce-scatter.8.cloned.1.call-done = bf16[96,768]{1,0:T(8,128)(2,1)} async-done(((bf16[3072,768]{1,0:T(8,128)(2,1)}), bf16[96,768]{1,0:T(8,128)(2,1)}) %reduce-scatter.8.cloned.1.call-update) | async-done | bytes 147472 | tf_op jit(solution)/shard_map/reduce_scatter | solution.py:946
  711.2 110.2 %reduce-scatter.6.cloned.1.call-done = bf16[24,3072]{1,0:T(8,128)(2,1)} async-done(((bf16[768,3072]{1,0:T(8,128)(2,1)}), bf16[24,3072]{1,0:T(8,128)(2,1)}) %reduce-scatter.6.cloned.1.call-update) | async-done | bytes 147472 | tf_op jit(solution)/shard_map/reduce_scatter | solution.py:945
  (166 shorter events, 48.3 us)
Async XLA Ops:
  7.2 292.7 %all-gather.4.cloned.1.call-start = ((), (), s32[]{:S(2)}) async-start(), calls=%async_computation.19 | async-start | bytes 4866048 | tf_op jit(solution)/shard_map/all_gather | solution.py:896
  15.7 51.3 %all-to-all-start.2 = ((bf16[8,3,5,16,384]{4,3,2,1,0:T(8,128)(2,1)}), bf16[8,3,5,16,384]{4,3,2,1,0:T(8,128)(2,1)S(1)}, u32[]{:S(2)}, u32[]{:S(2)}) async-start(bf16[8,3,5,16,384]{4,3,2,1,0:T(8,128)(2,1)} %get-tuple-element.78), calls=%async_computation.2 | async-start | bytes 2949120 | tf_op jit(solution)/shard_map/all_to_all | solution.py:848
  23.0 276.9 %all-gather.6.cloned.1.call-start = ((), (), s32[]{:S(2)}) async-start(), calls=%async_computation.20 | async-start | bytes 4866048 | tf_op jit(solution)/shard_map/all_gather | solution.py:897
  68.1 141.9 %all-to-all-start = ((bf16[8,3,5,16,384]{4,3,2,1,0:T(8,128)(2,1)}), bf16[8,3,5,16,384]{4,3,2,1,0:T(8,128)(2,1)}, u32[]{:S(2)}, u32[]{:S(2)}) async-start(bf16[8,3,5,16,384]{4,3,2,1,0:T(8,128)(2,1)} %get-tuple-element.76), calls=%async_computation | async-start | bytes 2949120 | tf_op jit(solution)/shard_map/all_to_all | solution.py:848
  210.0 17.3 %all-to-all-start.3 = ((bf16[8,5,16,384]{3,2,1,0:T(8,128)(2,1)}), bf16[8,5,16,384]{3,2,1,0:T(8,128)(2,1)S(1)}, u32[]{:S(2)}, u32[]{:S(2)}) async-start(bf16[8,5,16,384]{3,2,1,0:T(8,128)(2,1)} %get-tuple-element.79), calls=%async_computation.3 | async-start | bytes 983040 | tf_op jit(solution)/shard_map/all_to_all | solution.py:848
  213.5 31.5 %copy-start.18 = (bf16[8,5,16,384]{3,2,1,0:T(8,128)(2,1)S(1)}, bf16[8,5,16,384]{3,2,1,0:T(8,128)(2,1)}, u32[]{:S(2)}) copy-start(bf16[8,5,16,384]{3,2,1,0:T(8,128)(2,1)} %get-tuple-element.82) | copy-start | bytes 1474564
  227.3 33.9 %copy-start.19 = (bf16[8,5,16,384]{3,2,1,0:T(8,128)(2,1)S(1)}, bf16[8,5,16,384]{3,2,1,0:T(8,128)(2,1)}, u32[]{:S(2)}) copy-start(bf16[8,5,16,384]{3,2,1,0:T(8,128)(2,1)} %get-tuple-element.81) | copy-start | bytes 1474564
  227.3 50.8 %copy-start.6 = (bf16[8,5,16,384]{3,2,1,0:T(8,128)(2,1)}, bf16[8,5,16,384]{3,2,1,0:T(8,128)(2,1)S(1)}, u32[]{:S(2)}) copy-start(bf16[8,5,16,384]{3,2,1,0:T(8,128)(2,1)S(1)} %all-to-all-done.3.high_ref) | copy-start | bytes 1474564
  227.3 50.8 %copy-start.17 = (bf16[8,5,16,384]{3,2,1,0:T(8,128)(2,1)S(1)}, bf16[8,5,16,384]{3,2,1,0:T(8,128)(2,1)}, u32[]{:S(2)}) copy-start(bf16[8,5,16,384]{3,2,1,0:T(8,128)(2,1)} %get-tuple-element.85) | copy-start | bytes 1474564
  294.9 29.9 %all-to-all-start.6 = ((bf16[8,5,16,384]{3,2,1,0:T(8,128)(2,1)}), bf16[8,5,16,384]{3,2,1,0:T(8,128)(2,1)S(1)}, u32[]{:S(2)}, u32[]{:S(2)}) async-start(bf16[8,5,16,384]{3,2,1,0:T(8,128)(2,1)} %get-tuple-element.84), calls=%async_computation.6 | async-start | bytes 983040 | tf_op jit(solution)/shard_map/all_to_all | solution.py:848
  324.8 31.3 %copy-start.5 = (bf16[8,5,16,384]{3,2,1,0:T(8,128)(2,1)}, bf16[8,5,16,384]{3,2,1,0:T(8,128)(2,1)S(1)}, u32[]{:S(2)}) copy-start(bf16[8,5,16,384]{3,2,1,0:T(8,128)(2,1)S(1)} %all-to-all-done.6.low_ref) | copy-start | bytes 1474564
  324.8 31.3 %all-to-all-start.12 = ((bf16[8,5,16,384]{3,2,1,0:T(8,128)(2,1)}), bf16[8,5,16,384]{3,2,1,0:T(8,128)(2,1)S(1)}, u32[]{:S(2)}, u32[]{:S(2)}) async-start(bf16[8,5,16,384]{3,2,1,0:T(8,128)(2,1)} %get-tuple-element.97), calls=%async_computation.12 | async-start | bytes 983040 | tf_op jit(solution)/shard_map/all_to_all | solution.py:848
  331.0 43.4 %copy-start.16 = (bf16[8,5,16,384]{3,2,1,0:T(8,128)(2,1)S(1)}, bf16[8,5,16,384]{3,2,1,0:T(8,128)(2,1)}, u32[]{:S(2)}) copy-start(bf16[8,5,16,384]{3,2,1,0:T(8,128)(2,1)} %get-tuple-element.90) | copy-start | bytes 1474564
  356.1 34.5 %copy-start.4 = (bf16[8,5,16,384]{3,2,1,0:T(8,128)(2,1)}, bf16[8,5,16,384]{3,2,1,0:T(8,128)(2,1)S(1)}, u32[]{:S(2)}) copy-start(bf16[8,5,16,384]{3,2,1,0:T(8,128)(2,1)S(1)} %all-to-all-done.12.refs_0_) | copy-start | bytes 1474564
  390.6 28.8 %all-to-all-start.9 = ((bf16[8,5,16,384]{3,2,1,0:T(8,128)(2,1)}), bf16[8,5,16,384]{3,2,1,0:T(8,128)(2,1)S(1)}, u32[]{:S(2)}, u32[]{:S(2)}) async-start(bf16[8,5,16,384]{3,2,1,0:T(8,128)(2,1)} %get-tuple-element.91), calls=%async_computation.9 | async-start | bytes 983040 | tf_op jit(solution)/shard_map/all_to_all | solution.py:848
  438.3 23.6 %all-to-all-start.14 = ((bf16[8,5,16,384]{3,2,1,0:T(8,128)(2,1)}), bf16[8,5,16,384]{3,2,1,0:T(8,128)(2,1)S(1)}, u32[]{:S(2)}, u32[]{:S(2)}) async-start(bf16[8,5,16,384]{3,2,1,0:T(8,128)(2,1)} %get-tuple-element.99), calls=%async_computation.14 | async-start | bytes 983040 | tf_op jit(solution)/shard_map/all_to_all | solution.py:848
  441.9 157.6 %reduce-scatter.10.cloned.1.call-start = ((), (), s32[]{:S(2)}) async-start(), calls=%async_computation.23 | async-start | bytes 1216512
  488.1 221.0 %reduce-scatter.8.cloned.1.call-start = ((), (), s32[]{:S(2)}) async-start(), calls=%async_computation.22 | async-start | bytes 4866048 | tf_op jit(solution)/shard_map/reduce_scatter | solution.py:946
  503.4 318.1 %reduce-scatter.6.cloned.1.call-start = ((), (), s32[]{:S(2)}) async-start(), calls=%async_computation.21 | async-start | bytes 4866048 | tf_op jit(solution)/shard_map/reduce_scatter | solution.py:945
  564.8 39.0 %all-to-all-start.11 = ((bf16[8,3,5,16,384]{4,3,2,1,0:T(8,128)(2,1)}), bf16[8,3,5,16,384]{4,3,2,1,0:T(8,128)(2,1)S(1)}, u32[]{:S(2)}, u32[]{:S(2)}) async-start(bf16[8,3,5,16,384]{4,3,2,1,0:T(8,128)(2,1)} %get-tuple-element.96), calls=%async_computation.11 | async-start | bytes 2949120 | tf_op jit(solution)/shard_map/all_to_all | solution.py:848
  605.0 49.8 %copy-start.37 = (f32[312]{0:T(512)S(1)}, f32[312]{0:T(512)}, u32[]{:S(2)}) copy-start(f32[312]{0:T(512)} %param.32) | copy-start | bytes 3748
  605.0 49.8 %copy-start.38 = (f32[312]{0:T(512)S(1)}, f32[312]{0:T(512)}, u32[]{:S(2)}) copy-start(f32[312]{0:T(512)} %param.44) | copy-start | bytes 3748
  605.0 49.8 %copy-start.39 = (f32[312]{0:T(512)S(1)}, f32[312]{0:T(512)}, u32[]{:S(2)}) copy-start(f32[312]{0:T(512)} %param.39) | copy-start | bytes 3748
  605.0 49.8 %copy-start.40 = (f32[312]{0:T(512)S(1)}, f32[312]{0:T(512)}, u32[]{:S(2)}) copy-start(f32[312]{0:T(512)} %param.40) | copy-start | bytes 3748
  605.0 104.1 %copy-start.12 = (f32[96,768]{1,0:T(8,128)S(1)}, f32[96,768]{1,0:T(8,128)}, u32[]{:S(2)}) copy-start(f32[96,768]{1,0:T(8,128)} %param.31) | copy-start | bytes 884740
  605.0 104.1 %copy-start.20 = (f32[96,768]{1,0:T(8,128)S(1)}, f32[96,768]{1,0:T(8,128)}, u32[]{:S(2)}) copy-start(f32[96,768]{1,0:T(8,128)} %param.43) | copy-start | bytes 884740
  605.0 104.1 %copy-start.21 = (f32[96,768]{1,0:T(8,128)S(1)}, f32[96,768]{1,0:T(8,128)}, u32[]{:S(2)}) copy-start(f32[96,768]{1,0:T(8,128)} %param.37) | copy-start | bytes 884740
  605.0 104.1 %copy-start.22 = (f32[96,768]{1,0:T(8,128)S(1)}, f32[96,768]{1,0:T(8,128)}, u32[]{:S(2)}) copy-start(f32[96,768]{1,0:T(8,128)} %param.38) | copy-start | bytes 884740
  617.4 204.0 %copy-start.13 = (f32[24,3072]{1,0:T(8,128)S(1)}, f32[24,3072]{1,0:T(8,128)}, u32[]{:S(2)}) copy-start(f32[24,3072]{1,0:T(8,128)} %param.30) | copy-start | bytes 884740
  617.5 204.0 %copy-start.23 = (f32[24,3072]{1,0:T(8,128)S(1)}, f32[24,3072]{1,0:T(8,128)}, u32[]{:S(2)}) copy-start(f32[24,3072]{1,0:T(8,128)} %param.42) | copy-start | bytes 884740
  617.5 204.0 %copy-start.24 = (f32[24,3072]{1,0:T(8,128)S(1)}, f32[24,3072]{1,0:T(8,128)}, u32[]{:S(2)}) copy-start(f32[24,3072]{1,0:T(8,128)} %param.35) | copy-start | bytes 884740
  617.5 204.0 %copy-start.25 = (f32[24,3072]{1,0:T(8,128)S(1)}, f32[24,3072]{1,0:T(8,128)}, u32[]{:S(2)}) copy-start(f32[24,3072]{1,0:T(8,128)} %param.36) | copy-start | bytes 884740
  (28 other events, 179.1 us)
Sparse Core Ops, SparseCore 0:
  11.6 103.5 all-gather.3
  118.7 64.5 all-gather.5
  488.2 111.3 reduce-scatter.9
  604.9 104.1 reduce-scatter.7
  715.4 106.0 reduce-scatter.5

commit v2 on v1

--- a/solution.py
+++ b/solution.py
@@ -7,6 +7,7 @@
 from jax import lax
 from jax.experimental import pallas as pl
 from jax.experimental.pallas import tpu as pltpu
+from jax.sharding import Mesh
 from jax.sharding import PartitionSpec as P
 
 NB = 8
@@ -301,8 +302,15 @@
 SCHED = pltpu.CompilerParams(vmem_limit_bytes=VMEM_BYTES)
 
 
-def fits(parts):
-    return LAT % (parts * GROUP) == 0 and LON // 2 % (2 * parts) == 0
+def fits(sizes):
+    parts = sizes[1]
+    return sizes == (4, 8) and LAT % (parts * GROUP) == 0 and LON // 2 % (2 * parts) == 0
+
+
+def cost(time_us, bytes_moved):
+    return pl.CostEstimate(
+        flops=int(time_us * 1.15e9), bytes_accessed=bytes_moved, transcendentals=0
+    )
 
 
 def dot(left, right, left_dim, right_dim):
@@ -393,50 +401,81 @@
     return (center * inv_std, inv_std)
 
 
-def spread_body(tokens_ref, table_ref, low_ref, high_ref):
+def spread_body(tokens_ref, table_ref, filter_ref, small_ref, low_ref, high_ref):
+    step = pl.program_id(0)
     values = tokens_ref[...].astype(F32).reshape(GROUP * LON, 2 * HALF)
     normed, _ = normalise(values)
     out = dot(table_ref[...], normed.astype(BF16), 1, 0).astype(BF16)
-    low_ref[...] = out[:, :HALF].reshape(low_ref.shape)
-    high_ref[...] = out[:, HALF:].reshape(high_ref.shape)
-
-
-def spread(tokens, table, parts):
+    pairs = high_ref.shape[1]
+    parts = high_ref.shape[0]
+    units = low_ref.shape[1]
+    low_ref[:, pl.ds(step * pairs, pairs)] = out[:, :HALF].reshape(parts, pairs, 16, HALF)
+    high_ref[...] = out[:, HALF:].reshape(parts, pairs, 16, HALF)
+
+    @pl.when(step == 0)
+    def _():
+        rows = filter_ref.shape[0]
+        extra = units - pl.num_programs(0) * pairs
+        spare = jnp.zeros((16 * extra - rows - 1, HALF), F32)
+        own = jnp.concatenate([filter_ref[...], small_ref[...], spare], axis=0).astype(BF16)
+        own = own.reshape(1, extra, 16, HALF)
+        low_ref[:, units - extra :] = jnp.broadcast_to(own, (parts, extra, 16, HALF))
+
+
+def spread(tokens, table, filter_rows, small_row, parts):
     groups = tokens.shape[1] // GROUP
     pairs = LON // 4 // parts
-    shape = (parts, groups, pairs, 16, HALF)
-    block = pl.BlockSpec((parts, 1, pairs, 16, HALF), lambda r: (0, r, 0, 0, 0))
+    extra = filter_rows.shape[0] // 16 + 1
+    low = (parts, groups * pairs + extra, 16, HALF)
+    high = (parts, groups * pairs, 16, HALF)
+
+    def whole(*shape):
+        return pl.BlockSpec(shape, lambda r: (0,) * len(shape))
+
     return pl.pallas_call(
         spread_body,
         name="norm_and_longitude",
         grid=(groups,),
         in_specs=[
             pl.BlockSpec((1, GROUP, LON, 2 * HALF), lambda r: (0, r, 0, 0)),
-            pl.BlockSpec(table.shape, lambda r: (0, 0)),
+            whole(*table.shape),
+            whole(*filter_rows.shape),
+            whole(*small_row.shape),
         ],
-        out_specs=[block, block],
-        out_shape=[jax.ShapeDtypeStruct(shape, BF16)] * 2,
+        out_specs=[
+            whole(*low),
+            pl.BlockSpec((parts, pairs, 16, HALF), lambda r: (0, r, 0, 0)),
+        ],
+        out_shape=[jax.ShapeDtypeStruct(low, BF16), jax.ShapeDtypeStruct(high, BF16)],
         compiler_params=SCHED,
-    )(tokens, table)
+        cost_estimate=cost(7, 2 * tokens.size),
+    )(tokens, table, filter_rows, small_row)
+
+
+def unit_specs(parts, groups, pairs):
+    return [
+        pl.BlockSpec((parts, 1, 16, HALF), lambda b, pick_ref, r=r: (0, r * pairs + b, 0, 0))
+        for r in range(groups)
+    ]
+
+
+def stacked(refs):
+    return jnp.concatenate([ref[...] for ref in refs], axis=1).reshape(-1, HALF)
 
 
 def filter_body(
-    groups,
+    pieces,
     pick_ref,
-    arrived_ref,
-    forward_ref,
-    inverse_ref,
-    shift_row_ref,
-    params_ref,
-    one_ref,
-    two_ref,
-    *outs,
+    *refs,
 ):
-    back_refs = outs[:groups]
-    modes_ref, sums_ref, slopes_ref = outs[groups:]
+    arrived_refs = refs[: sum(pieces)]
+    forward_ref, inverse_ref, shift_row_ref, params_ref, one_ref, two_ref, *outs = refs[
+        sum(pieces) :
+    ]
+    back_refs = outs[:-3]
+    modes_ref, sums_ref, slopes_ref = outs[-3:]
     columns = forward_ref.shape[-1]
-    arrived = arrived_ref[...].reshape(columns, HALF)
-    raw = dot(forward_ref[0], arrived, 1, 0)
+    raw = dot(forward_ref[0], stacked(arrived_refs), 1, 0)
     gain = params_ref[0:1, :]
     shift = params_ref[1:2, :]
     modes_re = (raw[:ROWS] * gain + shift_row_ref[0, :, 0:1] * shift).astype(BF16)
@@ -469,14 +508,19 @@
     two_im = dot(sums_ref[0, 1], two_ref[0], 1, 0) + (two_bias_im - two_bias_im)
     both = jnp.concatenate([two_re.astype(BF16), two_im.astype(BF16)], axis=0)
     back = dot(inverse_ref[0], both, 1, 0).astype(BF16)
-    step = columns // groups
-    for group in range(groups):
-        ref = back_refs[group]
-        ref[...] = back[group * step : (group + 1) * step].reshape(ref.shape)
-
-
-def filter_forward(pick, arrived, tables, params, one, two, part_of_channels):
-    parts, groups, pairs = arrived.shape[:3]
+    step = columns // sum(pieces)
+    group = 0
+    for ref, count in zip(back_refs, pieces):
+        for place in range(count):
+            rows = back[group * step : (group + 1) * step]
+            ref[:, place] = rows.reshape(-1, 1, 16, HALF)
+            group += 1
+
+
+def filter_forward(pick, arrived, tables, params, one, two, part_of_channels, pieces):
+    parts = arrived.shape[0]
+    groups = sum(pieces)
+    pairs = LON // 4 // parts
     forward, inverse, _, _, shift_row = tables
     q = part_of_channels
     tall = 2 * ROWS
@@ -491,16 +535,20 @@
         zeros = (0,) * len(shape)
         return pl.BlockSpec((1,) + shape, lambda b, pick_ref: (b,) + zeros)
 
-    back_block = pl.BlockSpec((parts, 1, 16, HALF), lambda b, pick_ref: (0, b, 0, 0))
+    back_blocks = [
+        pl.BlockSpec((parts, count, 1, 16, HALF), lambda b, pick_ref: (0, 0, b, 0, 0))
+        for count in pieces
+    ]
+    back_shapes = [jax.ShapeDtypeStruct((parts, count, pairs, 16, HALF), BF16) for count in pieces]
     columns = forward.shape[-1]
     return pl.pallas_call(
-        functools.partial(filter_body, groups),
+        functools.partial(filter_body, pieces),
         name="filter_forward",
         grid_spec=pltpu.PrefetchScalarGridSpec(
             num_scalar_prefetch=1,
             grid=(pairs,),
-            in_specs=[
-                pl.BlockSpec((parts, groups, 1, 16, HALF), lambda b, pick_ref: (0, 0, b, 0, 0)),
+            in_specs=unit_specs(parts, groups, pairs)
+            + [
                 chosen(tall, columns),
                 chosen(columns, tall),
                 chosen(ROWS, 128),
@@ -508,17 +556,18 @@
                 fixed(HALF, 2 * HALF),
                 fixed(2 * HALF, HALF),
             ],
-            out_specs=[back_block] * groups
+            out_specs=back_blocks
             + [stepped(tall, HALF), stepped(2, ROWS, 2 * HALF), stepped(4, ROWS, HALF)],
         ),
-        out_shape=[jax.ShapeDtypeStruct((parts, pairs, 16, HALF), BF16)] * groups
+        out_shape=back_shapes
         + [
             jax.ShapeDtypeStruct((pairs, tall, HALF), BF16),
             jax.ShapeDtypeStruct((pairs, 2, ROWS, 2 * HALF), BF16),
             jax.ShapeDtypeStruct((pairs, 4, ROWS, HALF), BF16),
         ],
         compiler_params=SCHED,
-    )(pick, arrived, forward, inverse, shift_row, params, one, two)
+        cost_estimate=cost(14, 12 * 1024 * 1024),
+    )(pick, *[arrived] * groups, forward, inverse, shift_row, params, one, two)
 
 
 def filter_back_body(
@@ -527,10 +576,10 @@
     *refs,
 ):
     arrived_refs = refs[:groups]
-    adjoint_ref, inverse_ref, one_ref, two_ref, modes_ref, sums_ref, slopes_ref = refs[
-        groups : groups + 7
-    ]
-    sent_ref, one_grad_ref, two_grad_ref, bias_ref = refs[groups + 7 :]
+    adjoint_ref, inverse_ref, shift_row_ref, one_ref, two_ref = refs[groups : groups + 5]
+    normed_refs = refs[groups + 5 : 2 * groups + 5]
+    modes_ref, sums_ref, slopes_ref = refs[2 * groups + 5 : 2 * groups + 8]
+    sent_ref, one_grad_ref, two_grad_ref, bias_ref = refs[2 * groups + 8 :]
     columns = adjoint_ref.shape[-1]
     step = columns // groups
     arrived = jnp.concatenate([ref[...].reshape(step, HALF) for ref in arrived_refs], axis=0)
@@ -560,8 +609,13 @@
     sent_ref[...] = sent.reshape(sent_ref.shape)
     one_part = dot(modes_ref[0, :ROWS], out_re, 0, 0) + dot(modes_ref[0, ROWS:], out_im, 0, 0)
     two_part = dot(sums_ref[0, 0], grad_re, 0, 0) + dot(sums_ref[0, 1], grad_im, 0, 0)
-    rows = [jnp.sum(part, axis=0, keepdims=True) for part in (re_a, re_b, grad[:ROWS], grad[ROWS:])]
-    bias_part = jnp.concatenate(rows + [jnp.zeros((4, HALF), F32)], axis=0)
+    gain_part = sent.astype(F32) * stacked(normed_refs).astype(F32)
+    shift_part = modes_re * shift_row_ref[0, :, 0:1]
+    rows = [
+        jnp.sum(part, axis=0, keepdims=True)
+        for part in (re_a, re_b, grad[:ROWS], grad[ROWS:], gain_part, shift_part)
+    ]
+    bias_part = jnp.concatenate(rows + [jnp.zeros((2, HALF), F32)], axis=0)
     first = pl.program_id(0) == 0
 
     @pl.when(first)
@@ -577,10 +631,10 @@
         bias_ref[...] += bias_part
 
 
-def filter_backward(pick, arrived, tables, one, two, modes, sums, slopes, part_of_channels):
+def filter_backward(pick, arrived, tables, one, two, normed, modes, sums, slopes, part_of_channels):
     groups = len(arrived)
     parts, pairs = arrived[0].shape[:2]
-    _, _, adjoint, inverse, _ = tables
+    _, _, adjoint, inverse, shift_row = tables
     q = part_of_channels
     tall = 2 * ROWS
     columns = adjoint.shape[-1]
@@ -598,7 +652,7 @@
     def whole(*shape):
         return pl.BlockSpec(shape, lambda b, pick_ref: (0,) * len(shape))
 
-    arrived_block = pl.BlockSpec((parts, 1, 16, HALF), lambda b, pick_ref: (0, b, 0, 0))
+    arrived_block = pl.BlockSpec((parts, 1, 16, HALF), lambda b, pick_ref: (0, b, 0, q))
     return pl.pallas_call(
         functools.partial(filter_back_body, groups),
         name="filter_backward",
@@ -609,8 +663,12 @@
             + [
                 chosen(tall, columns),
                 chosen(columns, tall),
+                chosen(ROWS, 128),
                 fixed(HALF, 2 * HALF),
                 fixed(2 * HALF, HALF),
+            ]
+            + unit_specs(parts, groups, pairs)
+            + [
                 stepped(tall, HALF),
                 stepped(2, ROWS, 2 * HALF),
                 stepped(4, ROWS, HALF),
@@ -629,7 +687,8 @@
             jax.ShapeDtypeStruct((8, HALF), F32),
         ],
         compiler_params=SCHED,
-    )(pick, *arrived, adjoint, inverse, one, two, modes, sums, slopes)
+        cost_estimate=cost(18, 12 * 1024 * 1024),
+    )(pick, *arrived, adjoint, inverse, shift_row, one, two, *[normed] * groups, modes, sums, slopes)
 
 
 def dense_body(
@@ -643,20 +702,22 @@
     in_bias_ref,
     in_ref,
     out_ref,
-    result_ref,
-    mixed_grad_ref,
-    low_sent_ref,
-    high_sent_ref,
-    second_ref,
-    grad_low_ref,
-    act_ref,
-    grad_pre_ref,
-    in_bias_grad_ref,
-    rows_ref,
-    mixed_ref,
-    branch_ref,
-    grad_second_ref,
+    *refs,
 ):
+    (
+        result_ref,
+        mixed_grad_ref,
+        second_ref,
+        grad_low_ref,
+        act_ref,
+        grad_pre_ref,
+        sent_ref,
+        in_bias_grad_ref,
+        rows_ref,
+        mixed_ref,
+        branch_ref,
+        grad_second_ref,
+    ) = refs[-12:]
     chunk = pl.program_id(0)
     count = GROUP * LON
     wide = 2 * HALF
@@ -709,14 +770,20 @@
             jnp.sum(part, axis=0, keepdims=True)
             for part in (upstream * normed_two, upstream, grad_low_ref[...].astype(F32))
         ]
-        rows_ref[...] = jnp.concatenate(rows + [jnp.zeros((5, wide), F32)], axis=0)
+        normed_one, _ = normalise(tokens_ref[...].astype(F32).reshape(count, wide))
+        rows += [
+            jnp.sum(part, axis=0, keepdims=True) for part in (mixed_grad * normed_one, mixed_grad)
+        ]
+        rows_ref[...] = jnp.concatenate(rows + [jnp.zeros((3, wide), F32)], axis=0)
         sent = dot(table_ref[...], mixed_grad.astype(BF16), 1, 0).astype(BF16)
-        low_sent_ref[...] = sent[:, :HALF].reshape(low_sent_ref.shape)
-        high_sent_ref[...] = sent[:, HALF:].reshape(high_sent_ref.shape)
-
-
-def dense(tokens, cotangent, low, high, inverse, table, params, in_bias, in_work, out_work, group):
-    parts, pairs = low.shape[:2]
+        sent_ref[...] = sent.reshape(sent_ref.shape)
+
+
+def dense(
+    kept, tokens, cotangent, low, high, places, inverse, table, params, in_bias, in_work, out_work, group
+):
+    parts, _, pairs = high.shape[:3]
+    groups = tokens.shape[1] // GROUP
     count = GROUP * LON
     wide = 2 * HALF
     hidden = in_work.shape[1]
@@ -724,64 +791,65 @@
     def whole(*shape):
         return pl.BlockSpec(shape, lambda f: (0,) * len(shape))
 
-    rows_in = pl.BlockSpec((1, GROUP, LON, wide), lambda f: (0, group, 0, 0))
-    sent = whole(parts, pairs, 16, HALF)
+    rows = pl.BlockSpec((1, GROUP, LON, wide), lambda f: (0, group, 0, 0))
+    low_spec, high_spec = (
+        pl.BlockSpec((parts, 1, pairs, 16, HALF), lambda f, place=place: (0, place, 0, 0, 0))
+        for place in places
+    )
+    token_rows = pl.BlockSpec((count, wide), lambda f: (group, 0))
+    hidden_rows = pl.BlockSpec((count, FCHUNK), lambda f: (group, f))
     return pl.pallas_call(
         dense_body,
         name="dense_group",
         grid=(hidden // FCHUNK,),
         in_specs=[
-            rows_in,
-            rows_in,
-            sent,
-            sent,
+            rows,
+            rows,
+            low_spec,
+            high_spec,
             whole(*inverse.shape),
             whole(*table.shape),
             whole(16, wide),
             pl.BlockSpec((1, FCHUNK), lambda f: (0, f)),
             pl.BlockSpec((wide, FCHUNK), lambda f: (0, f)),
             pl.BlockSpec((FCHUNK, wide), lambda f: (f, 0)),
-        ],
+        ]
+        + [pl.BlockSpec(memory_space=pl.ANY)] * len(kept),
         out_specs=[
-            whole(GROUP, LON, wide),
-            whole(GROUP, LON, wide),
-            sent,
-            sent,
-            whole(count, wide),
-            whole(count, wide),
-            pl.BlockSpec((count, FCHUNK), lambda f: (0, f)),
-            pl.BlockSpec((count, FCHUNK), lambda f: (0, f)),
+            rows,
+            rows,
+            token_rows,
+            token_rows,
+            hidden_rows,
+            hidden_rows,
+            whole(parts, pairs, 16, wide),
             pl.BlockSpec((1, FCHUNK), lambda f: (0, f)),
             whole(8, wide),
         ],
         out_shape=[
-            jax.ShapeDtypeStruct((GROUP, LON, wide), BF16),
-            jax.ShapeDtypeStruct((GROUP, LON, wide), F32),
-            jax.ShapeDtypeStruct((parts, pairs, 16, HALF), BF16),
-            jax.ShapeDtypeStruct((parts, pairs, 16, HALF), BF16),
-            jax.ShapeDtypeStruct((count, wide), BF16),
-            jax.ShapeDtypeStruct((count, wide), BF16),
-            jax.ShapeDtypeStruct((count, hidden), BF16),
-            jax.ShapeDtypeStruct((count, hidden), BF16),
+            jax.ShapeDtypeStruct(tokens.shape, BF16),
+            jax.ShapeDtypeStruct(tokens.shape, F32),
+            jax.ShapeDtypeStruct((groups * count, wide), BF16),
+            jax.ShapeDtypeStruct((groups * count, wide), BF16),
+            jax.ShapeDtypeStruct((groups * count, hidden), BF16),
+            jax.ShapeDtypeStruct((groups * count, hidden), BF16),
+            jax.ShapeDtypeStruct((parts, pairs, 16, wide), BF16),
             jax.ShapeDtypeStruct((1, hidden), F32),
             jax.ShapeDtypeStruct((8, wide), F32),
         ],
         scratch_shapes=[pltpu.VMEM((count, wide), F32)] * 3,
+        input_output_aliases={10 + i: i for i in range(len(kept))},
         compiler_params=SCHED,
-    )(tokens, cotangent, low, high, inverse, table, params, in_bias, in_work, out_work)
-
-
-def gather_grad_body(groups, *refs):
-    tokens_ref = refs[0]
-    mixed_grad_refs = refs[1 : 1 + groups]
-    low_ref, high_ref, inverse_ref, params_ref, grad_ref, rows_ref = refs[1 + groups :]
-    step = pl.program_id(0)
+        cost_estimate=cost(25, 30 * 1024 * 1024),
+    )(tokens, cotangent, low, high, inverse, table, params, in_bias, in_work, out_work, *kept)
+
+
+def gather_grad_body(
+    tokens_ref, mixed_grad_ref, low_ref, high_ref, inverse_ref, params_ref, grad_ref
+):
     count = GROUP * LON
     wide = 2 * HALF
-    mixed_grad = mixed_grad_refs[0][...]
-    for group in range(1, groups):
-        mixed_grad = jnp.where(step == group, mixed_grad_refs[group][...], mixed_grad)
-    mixed_grad = mixed_grad.reshape(count, wide)
+    mixed_grad = mixed_grad_ref[...].reshape(count, wide)
     low = dot(inverse_ref[...], low_ref[...].reshape(count, HALF), 1, 0)
     high = dot(inverse_ref[...], high_ref[...].reshape(count, HALF), 1, 0)
     upstream = mixed_grad + jnp.concatenate([low, high], axis=1)
@@ -791,19 +859,9 @@
     second_mean = jnp.mean(scaled * normed, axis=-1, keepdims=True)
     out = mixed_grad + inv_std * (scaled - first_mean - normed * second_mean)
     grad_ref[...] = out.reshape(grad_ref.shape)
-    rows = [jnp.sum(part, axis=0, keepdims=True) for part in (upstream * normed, upstream)]
-    part = jnp.concatenate(rows + [jnp.zeros((6, wide), F32)], axis=0)
-
-    @pl.when(step == 0)
-    def _():
-        rows_ref[...] = part
-
-    @pl.when(step > 0)
-    def _():
-        rows_ref[...] += part
-
-
-def gather_grad(tokens, mixed_grads, low, high, inverse, params):
+
+
+def gather_grad(tokens, mixed_grad, low, high, inverse, params):
     parts, groups, pairs = low.shape[:3]
     wide = 2 * HALF
 
@@ -813,28 +871,36 @@
     rows = pl.BlockSpec((1, GROUP, LON, wide), lambda r: (0, r, 0, 0))
     arrived = pl.BlockSpec((parts, 1, pairs, 16, HALF), lambda r: (0, r, 0, 0, 0))
     return pl.pallas_call(
-        functools.partial(gather_grad_body, groups),
+        gather_grad_body,
         name="longitude_and_norm_grad",
         grid=(groups,),
-        in_specs=[rows]
-        + [whole(GROUP, LON, wide)] * groups
-        + [arrived, arrived, whole(*inverse.shape), whole(16, wide)],
-        out_specs=[rows, whole(8, wide)],
-        out_shape=[
-            jax.ShapeDtypeStruct((1, groups * GROUP, LON, wide), F32),
-            jax.ShapeDtypeStruct((8, wide), F32),
-        ],
+        in_specs=[rows, rows, arrived, arrived, whole(*inverse.shape), whole(16, wide)],
+        out_specs=rows,
+        out_shape=jax.ShapeDtypeStruct((1, groups * GROUP, LON, wide), F32),
         compiler_params=SCHED,
-    )(tokens, *mixed_grads, low, high, inverse, params)
+        cost_estimate=cost(12, 16 * 1024 * 1024),
+    )(tokens, mixed_grad, low, high, inverse, params)
 
 
 def block_matrices(weight):
-    size = weight.shape[1] // 2
-    count = HALF // size
-    grouped = weight.reshape(2, count, size, 2, size)
-    eye = jnp.eye(count, dtype=weight.dtype)
-    full = grouped[:, :, :, :, None, :] * eye[None, :, None, None, :, None]
-    return full.reshape(2, HALF, 2, HALF)
+    size = weight.shape[1] // 4
+    places = np.arange(HALF)
+    pick = (np.arange(4 * size)[:, None, None] == np.arange(4)[:, None] * size + places % size)
+    own = places[:, None] // size == places[None, :] // size
+    halves = weight.reshape(2, HALF, 4 * size)
+
+    def spread_columns(form, first):
+        full = jnp.einsum(
+            form, halves, jnp.asarray(pick[:, first : first + 2], BF16), preferred_element_type=F32
+        )
+        return full
+
+    one = spread_columns("qrc,cpn->qrpn", 0) * own[:, None, :]
+    two = spread_columns("qrc,cpn->qprn", 2) * own
+    return (
+        one.astype(BF16).reshape(2, HALF, 2 * HALF),
+        two.astype(BF16).reshape(2, 2 * HALF, HALF),
+    )
 
 
 def own_blocks(matrix, size):
@@ -844,8 +910,209 @@
     )
 
 
-def exchange(values):
+def in_turn(values, last):
+    return lax.optimization_barrier((values, last))[0]
+
+
+def exchange(values, last=None):
+    if last is not None:
+        values = in_turn(values, last)
     return lax.all_to_all(values, "sp", split_axis=0, concat_axis=0, tiled=True)
+
+
+AXES = ("y", "core", "sp")
+BITS = (("y", 1), ("core", 1), ("sp", 4), ("sp", 2), ("sp", 1))
+SIZES = {"y": 2, "core": 2, "sp": 8}
+
+
+def swap(values, axis, bit):
+    return lax.ppermute(values, axis, [(i, i ^ bit) for i in range(SIZES[axis])])
+
+
+def mine(axis, bit):
+    return (lax.axis_index(axis) // bit) % 2
+
+
+def gather_bit(values, axis, bit):
+    other = swap(values, axis, bit)
+    low = mine(axis, bit) == 0
+    return jnp.stack([jnp.where(low, values, other), jnp.where(low, other, values)])
+
+
+def scatter_bits(values, order, late, last):
+    held = list(BITS)
+    values = values.reshape((2,) * len(held) + values.shape[1:])
+    for step, (axis, bit) in enumerate(order):
+        if step == late:
+            values = in_turn(values, last)
+        place = held.index((axis, bit))
+        keep = lax.dynamic_index_in_dim(values, mine(axis, bit), place, keepdims=False)
+        give = lax.dynamic_index_in_dim(values, 1 - mine(axis, bit), place, keepdims=False)
+        values = keep + swap(give, axis, bit)
+        held.pop(place)
+    return values
+
+
+SMALL = pl.CostEstimate(flops=1 << 20, bytes_accessed=1 << 20, transcendentals=0)
+IN_ORDER = (("core", 1), ("y", 1), ("sp", 1), ("sp", 2), ("sp", 4))
+OUT_ORDER = (("core", 1), ("sp", 1), ("y", 1), ("sp", 2), ("sp", 4))
+
+
+def device_rows(order):
+    lists = []
+    for core in range(2):
+        indices = []
+        for count in range(16):
+            samp, sp = core, 0
+            for place, (axis, bit) in enumerate(order[1:]):
+                if count >> (3 - place) & 1:
+                    samp, sp = (samp + 2 * bit, sp) if axis == "y" else (samp, sp + bit)
+            indices.append(samp * 8 + sp)
+        lists.append(indices)
+    return lists
+
+
+def in_weight_grad_body(pick_ref, second_ref, grad_pre_ref, keep_ref, give_ref):
+    out = dot(second_ref[...], grad_pre_ref[...], 0, 0)
+    rows = out.shape[0] // 32
+    halves = [
+        jnp.concatenate([out[i * rows : (i + 1) * rows] for i in indices], axis=0).astype(BF16)
+        for indices in device_rows(IN_ORDER)
+    ]
+
+    @pl.when(pick_ref[0] == 0)
+    def _():
+        keep_ref[...] = halves[0]
+        give_ref[...] = halves[1]
+
+    @pl.when(pick_ref[0] == 1)
+    def _():
+        keep_ref[...] = halves[1]
+        give_ref[...] = halves[0]
+
+
+def in_weight_grad(core, second, grad_pre):
+    tokens, wide = second.shape
+    hidden = grad_pre.shape[1]
+    step = 512
+    half = pl.BlockSpec((wide // 2, step), lambda i, pick_ref: (0, i))
+    return pl.pallas_call(
+        in_weight_grad_body,
+        name="in_weight_grad",
+        grid_spec=pltpu.PrefetchScalarGridSpec(
+            num_scalar_prefetch=1,
+            grid=(hidden // step,),
+            in_specs=[
+                pl.BlockSpec((tokens, wide), lambda i, pick_ref: (0, 0)),
+                pl.BlockSpec((tokens, step), lambda i, pick_ref: (0, i)),
+            ],
+            out_specs=[half, half],
+        ),
+        out_shape=[jax.ShapeDtypeStruct((wide // 2, hidden), BF16)] * 2,
+        compiler_params=SCHED,
+        cost_estimate=SMALL,
+    )(core, second, grad_pre)
+
+
+def out_weight_grad_body(pick_ref, act_ref, grad_low_ref, keep_ref, give_ref):
+    out = dot(act_ref[...], grad_low_ref[...], 0, 0)
+    rows = out.shape[0] // 8
+    out = out.astype(BF16)
+    pieces = [
+        jnp.concatenate(
+            [
+                out[(z1 * 4 + z0 * 2 + x) * rows : (z1 * 4 + z0 * 2 + x + 1) * rows]
+                for z0 in range(2)
+                for z1 in range(2)
+            ],
+            axis=0,
+        )
+        for x in range(2)
+    ]
+
+    @pl.when(pl.program_id(0) == 0)
+    def _():
+        for x in range(2):
+            keep_ref[x, 0] = pieces[x]
+
+    @pl.when(pl.program_id(0) == 1)
+    def _():
+        for x in range(2):
+            give_ref[x, 0] = pieces[x]
+
+
+def out_weight_grad(core, act, grad_low):
+    tokens, hidden = act.shape
+    wide = grad_low.shape[1]
+    part = hidden // 4
+    shape = (2, 2, part // 2, wide)
+
+    def columns(give, y, pick_ref):
+        return (0, y * 2 + (pick_ref[0] + give) % 2)
+
+    keep, give = pl.pallas_call(
+        out_weight_grad_body,
+        name="out_weight_grad",
+        grid_spec=pltpu.PrefetchScalarGridSpec(
+            num_scalar_prefetch=1,
+            grid=(2, 2),
+            in_specs=[
+                pl.BlockSpec((tokens, part), columns),
+                pl.BlockSpec((tokens, wide), lambda give, y, pick_ref: (0, 0)),
+            ],
+            out_specs=[
+                pl.BlockSpec(
+                    (2, 1) + shape[2:], lambda give, y, pick_ref: (0, jnp.maximum(y, give), 0, 0)
+                ),
+                pl.BlockSpec((2, 1) + shape[2:], lambda give, y, pick_ref: (0, y * give, 0, 0)),
+            ],
+        ),
+        out_shape=[jax.ShapeDtypeStruct(shape, BF16)] * 2,
+        compiler_params=SCHED,
+        cost_estimate=SMALL,
+    )(core, act, grad_low)
+    return keep.reshape(-1, wide), give.reshape(-1, wide)
+
+
+def add_split_body(pick_ref, keep_one, got_one, keep_two, got_two, keep_ref, give_ref):
+    keep_ref[...] = (keep_one[...].astype(F32) + got_one[...].astype(F32)).astype(BF16)
+    give_ref[...] = (keep_two[...].astype(F32) + got_two[...].astype(F32)).astype(BF16)
+
+
+def add_split(pick, keep, got):
+    rows, columns = keep.shape
+    steps = 2 if rows % 64 == 0 else 1
+    block = (rows // 2 // steps, columns)
+    stays = pl.BlockSpec(block, lambda i, pick_ref: (pick_ref[0] * steps + i, 0))
+    goes = pl.BlockSpec(block, lambda i, pick_ref: ((1 - pick_ref[0]) * steps + i, 0))
+    out = pl.BlockSpec(block, lambda i, pick_ref: (i, 0))
+    return pl.pallas_call(
+        add_split_body,
+        name="add_split",
+        grid_spec=pltpu.PrefetchScalarGridSpec(
+            num_scalar_prefetch=1,
+            grid=(steps,),
+            in_specs=[stays, stays, goes, goes],
+            out_specs=[out, out],
+        ),
+        out_shape=[jax.ShapeDtypeStruct((rows // 2, columns), BF16)] * 2,
+        compiler_params=SCHED,
+        cost_estimate=SMALL,
+    )(pick, keep, got, keep, got)
+
+
+def picks(order):
+    return [mine(axis, bit).astype(jnp.int32).reshape(1) for axis, bit in order]
+
+
+def scatter_steps(keep, give, order, chosen, first, last):
+    for place in range(first, last):
+        keep, give = add_split(chosen[place + 1], keep, swap(give, *order[place]))
+    return keep, give
+
+
+def scatter_last(keep, give, order):
+    return keep.astype(F32) + swap(give, *order[-1]).astype(F32)
 
 
 def fast_shards(
@@ -870,7 +1137,6 @@
     out_ema,
     small_ema,
 ):
-    both = ("samp", "sp")
     parts = sizes[1]
     devices = sizes[0] * sizes[1]
     groups = tokens.shape[1] // GROUP
@@ -887,14 +1153,29 @@
     pick = jnp.where((sp_index == 0) & (jnp.arange(pairs) == 0), 0, 1).astype(jnp.int32)
 
     filter_rows = filter_master.shape[0]
-    small_line = jnp.pad(small_master.astype(BF16), (0, 4 * block - small_share)).reshape(1, -1)
-    packed = jnp.concatenate([filter_master.astype(BF16), small_line], axis=0)
-    sent = spread(tokens, lon_table, parts)
-    packed_all = lax.all_gather(packed, both, axis=0, tiled=True).reshape(devices, filter_rows + 1, -1)
+    small_row = jnp.pad(small_master, (0, 4 * block - small_share)).reshape(1, -1)
+    sent = spread(tokens, lon_table, filter_master, small_row, parts)
+    arrived_low = exchange(sent[0])
+    arrived_high = exchange(sent[1], arrived_low)
+
+    units = groups * pairs
+    near = arrived_low[:, units:].reshape(parts, -1, 4 * block)
+    packed_all = gather_bit(gather_bit(near, "core", 1), "y", 1)
+    packed_all = packed_all.reshape((devices,) + near.shape[1:])
     filter_work = packed_all[:, :filter_rows].reshape(width, 4 * block)
     small_work = packed_all[:, filter_rows, :small_share].reshape(-1)
-    in_work = lax.all_gather(in_master.astype(BF16), both, axis=0, tiled=True)
-    out_work = lax.all_gather(out_master.astype(BF16), both, axis=0, tiled=True)
+
+    in_rows, hidden = in_master.shape
+    chunks = hidden // width
+    in_line, out_line = in_turn((in_master, out_master), sent[0])
+    in_block = in_line.astype(BF16).reshape(in_rows, chunks, width).transpose(1, 0, 2)
+    dense_block = jnp.concatenate(
+        [in_block.reshape(in_rows * chunks, width), out_line.astype(BF16)], axis=0
+    )
+    dense_all = lax.all_gather(dense_block, AXES, axis=0, tiled=False)
+    in_work = dense_all[:, : in_rows * chunks].reshape(devices, chunks, in_rows, width)
+    in_work = in_work.transpose(0, 2, 1, 3).reshape(width, hidden)
+    out_work = dense_all[:, in_rows * chunks :].reshape(hidden, width)
 
     params = small_work.astype(F32).reshape(13, width)
     scale = storm_weight.astype(F32)[0] / 64.0
@@ -902,20 +1183,30 @@
     params = jnp.concatenate(
         [params, jnp.full((1, width), scale, F32), jnp.zeros((2, width), F32)], axis=0
     )
-    one = block_matrices(filter_work[:, : 2 * block]).reshape(2, HALF, 2 * HALF)
-    two = block_matrices(filter_work[:, 2 * block :]).transpose(0, 2, 1, 3).reshape(2, 2 * HALF, HALF)
-
-    arrived = [exchange(piece) for piece in sent]
-    forward = [
-        filter_forward(pick, arrived[q], tables, params, one, two, q) for q in range(2)
-    ]
-    returned = [[exchange(forward[q][group]) for q in range(2)] for group in range(groups)]
-    dense_out = [
-        dense(
+    one, two = block_matrices(filter_work)
+
+    forward_low = filter_forward(pick, arrived_low, tables, params, one, two, 0, (groups,))
+    returned_low = exchange(forward_low[0], arrived_high)
+    high_pieces = (1, groups - 1) if groups > 1 else (1,)
+    forward_high = filter_forward(pick, arrived_high, tables, params, one, two, 1, high_pieces)
+    last = (returned_low, in_work, out_work)
+    returned_high = []
+    for piece in range(len(high_pieces)):
+        last = exchange(forward_high[piece], last)
+        returned_high.append(last)
+    kept = []
+    grad_arrived = []
+    dense_rows = 0.0
+    in_bias_grad = 0.0
+    for group in range(groups):
+        piece = min(group, 1)
+        *kept, sent_piece, bias_piece, rows_piece = dense(
+            kept,
             tokens,
             cotangent,
-            returned[group][0],
-            returned[group][1],
+            returned_low,
+            returned_high[piece],
+            (group, group - piece),
             lon_back,
             lon_table,
             params,
@@ -924,31 +1215,50 @@
             out_work,
             group,
         )
-        for group in range(groups)
-    ]
-    grad_arrived = [[exchange(dense_out[group][2 + q]) for group in range(groups)] for q in range(2)]
-    backward = [
-        filter_backward(pick, grad_arrived[q], tables, one, two, *forward[q][groups:], q)
-        for q in range(2)
-    ]
-    grad_returned = [exchange(backward[q][0]) for q in range(2)]
-    input_grad, norm_rows = gather_grad(
-        tokens, [part[1] for part in dense_out], grad_returned[0], grad_returned[1], lon_back, params
-    )
-    result = jnp.concatenate([part[0] for part in dense_out], axis=0)[None]
-
-    second, grad_low, act, grad_pre = (
-        jnp.concatenate([part[i] for part in dense_out], axis=0) for i in (4, 5, 6, 7)
-    )
-    out_local = jnp.einsum("tf,td->fd", act, grad_low, preferred_element_type=F32).astype(BF16)
-    in_local = jnp.einsum("td,tf->df", second, grad_pre, preferred_element_type=F32).astype(BF16)
-    in_grad = lax.psum_scatter(in_local, both, scatter_dimension=0, tiled=True).astype(F32)
-    out_grad = lax.psum_scatter(out_local, both, scatter_dimension=0, tiled=True).astype(F32)
+        in_bias_grad = in_bias_grad + bias_piece
+        dense_rows = dense_rows + rows_piece
+        before_last = last
+        last = exchange(sent_piece, last)
+        grad_arrived.append(last)
+    result, mixed_grad, second, grad_low, act, grad_pre = kept
+    act, grad_pre = in_turn((act, grad_pre), before_last)
+    in_picks, out_picks = picks(IN_ORDER), picks(OUT_ORDER)
+    out_part, in_part = in_turn(
+        (
+            out_weight_grad(out_picks[0], act, grad_low),
+            in_weight_grad(in_picks[0], second, grad_pre),
+        ),
+        last,
+    )
+    out_part = scatter_steps(*out_part, OUT_ORDER, out_picks, 0, 1)
+    in_part = scatter_steps(*in_part, IN_ORDER, in_picks, 0, 1)
+
+    backward = []
+    grad_returned = []
+    for q, (normed, forward) in enumerate(
+        ((arrived_low, forward_low), (arrived_high, forward_high))
+    ):
+        if q == 1:
+            grad_arrived = in_turn(grad_arrived, (in_part, out_part))
+        backward.append(
+            filter_backward(pick, grad_arrived, tables, one, two, normed, *forward[-3:], q)
+        )
+        if q == 1:
+            out_part = scatter_steps(*out_part, OUT_ORDER, out_picks, 1, 2)
+            in_part = scatter_steps(*in_part, IN_ORDER, in_picks, 1, 2)
+            last = (last, out_part, in_part)
+        last = exchange(backward[q][0], last)
+        grad_returned.append(last)
+
+    out_part = scatter_steps(*out_part, OUT_ORDER, out_picks, 2, 4)
+    in_part = scatter_steps(*in_part, IN_ORDER, in_picks, 2, 4)
+    out_part, in_part = in_turn((out_part, in_part), last)
+    out_grad = scatter_last(*out_part, OUT_ORDER)
+    in_grad = scatter_last(*in_part, IN_ORDER)
 
     pieces = []
     for q in range(2):
-        one_grad = backward[q][1]
-        two_grad = backward[q][2]
+        one_grad, two_grad = in_turn((backward[q][1], backward[q][2]), grad_returned[0])
         pieces.append(
             jnp.concatenate(
                 [
@@ -960,15 +1270,11 @@
                 axis=1,
             )
         )
-    filter_local = jnp.concatenate(pieces, axis=0)
-    filter_grad = lax.psum_scatter(filter_local, both, scatter_dimension=0, tiled=True)
-
+    filter_local = jnp.concatenate(pieces, axis=0).reshape(devices, filter_rows, 4 * block)
     bias_rows = jnp.concatenate([backward[0][3], backward[1][3]], axis=1)
-    dense_rows = sum(part[9] for part in dense_out)
-    in_bias_grad = sum(part[8] for part in dense_out)
-    small_local = jnp.concatenate(
+    small_rows = jnp.concatenate(
         [
-            norm_rows[0:2],
+            dense_rows[3:5] + bias_rows[4:6],
             dense_rows[0:2],
             bias_rows[0:2],
             bias_rows[2:3] + bias_rows[2:3],
@@ -977,8 +1283,27 @@
             in_bias_grad.reshape(4, width),
         ],
         axis=0,
-    ).reshape(-1)
-    small_grad = lax.psum_scatter(small_local, both, scatter_dimension=0, tiled=True)
+    )
+
+    def shares(rows):
+        flat = rows.reshape(-1)
+        flat = jnp.pad(flat, (0, devices * small_share - flat.shape[0]))
+        return jnp.pad(flat.reshape(devices, small_share), ((0, 0), (0, 4 * block - small_share)))
+
+    early = scatter_bits(
+        jnp.concatenate([filter_local, shares(small_rows)[:, None]], axis=1), IN_ORDER, 3, last
+    )
+    filter_grad = early[:filter_rows]
+    small_grad = early[filter_rows, :small_share]
+
+    input_grad = gather_grad(
+        tokens,
+        mixed_grad,
+        grad_returned[0],
+        grad_returned[1],
+        lon_back,
+        params,
+    )
 
     filter_new, filter_m_new, filter_v_new, filter_ema_new = adam_update(
         filter_master, filter_grad, filter_m, filter_v, filter_ema, 0.2
@@ -1020,54 +1345,60 @@
 
 def solution(mesh):
     sizes = (mesh.shape["samp"], mesh.shape["sp"])
-    body = functools.partial(fast_shards, sizes) if fits(sizes[1]) else plain_shards
+    samp = "samp"
+    body = plain_shards
+    if fits(sizes):
+        samp = ("y", "core")
+        mesh = Mesh(mesh.devices.reshape(2, 2, sizes[1]), AXES)
+        body = functools.partial(fast_shards, sizes)
+    every = (*samp, "sp") if isinstance(samp, tuple) else (samp, "sp")
     return jax.shard_map(
         body,
         mesh=mesh,
         in_specs=(
-            P("samp", "sp", None, None),
-            P("samp", "sp", None, None),
-            P("samp"),
-            P(("samp", "sp"), None),
-            P(("samp", "sp"), None),
-            P(("samp", "sp"), None),
-            P(("samp", "sp")),
-            P(("samp", "sp"), None),
-            P(("samp", "sp"), None),
-            P(("samp", "sp"), None),
-            P(("samp", "sp"), None),
-            P(("samp", "sp"), None),
-            P(("samp", "sp"), None),
-            P(("samp", "sp")),
-            P(("samp", "sp")),
-            P(("samp", "sp"), None),
-            P(("samp", "sp"), None),
-            P(("samp", "sp"), None),
-            P(("samp", "sp")),
+            P(samp, "sp", None, None),
+            P(samp, "sp", None, None),
+            P(samp),
+            P(every, None),
+            P(every, None),
+            P(every, None),
+            P(every),
+            P(every, None),
+            P(every, None),
+            P(every, None),
+            P(every, None),
+            P(every, None),
+            P(every, None),
+            P(every),
+            P(every),
+            P(every, None),
+            P(every, None),
+            P(every, None),
+            P(every),
         ),
         out_specs=(
-            P("samp", "sp", None, None),
-            P("samp", "sp", None, None),
-            P(("samp", "sp"), None),
-            P(("samp", "sp"), None),
-            P(("samp", "sp"), None),
-            P(("samp", "sp")),
-            P(("samp", "sp"), None),
-            P(("samp", "sp"), None),
-            P(("samp", "sp"), None),
-            P(("samp", "sp")),
-            P(("samp", "sp"), None),
-            P(("samp", "sp"), None),
-            P(("samp", "sp"), None),
-            P(("samp", "sp"), None),
-            P(("samp", "sp"), None),
-            P(("samp", "sp"), None),
-            P(("samp", "sp")),
-            P(("samp", "sp")),
-            P(("samp", "sp"), None),
-            P(("samp", "sp"), None),
-            P(("samp", "sp"), None),
-            P(("samp", "sp")),
+            P(samp, "sp", None, None),
+            P(samp, "sp", None, None),
+            P(every, None),
+            P(every, None),
+            P(every, None),
+            P(every),
+            P(every, None),
+            P(every, None),
+            P(every, None),
+            P(every),
+            P(every, None),
+            P(every, None),
+            P(every, None),
+            P(every, None),
+            P(every, None),
+            P(every, None),
+            P(every),
+            P(every),
+            P(every, None),
+            P(every, None),
+            P(every, None),
+            P(every),
         ),
         check_vma=False,
     )

time: 840 us -> 502 us (0.60)
  blocking collectives: 311 us -> 65.6 us
  waiting for transfers between devices: 237 us -> 80.5 us
  Pallas kernels: 157 us -> 209 us
  starting transfers between devices: 37.8 us -> 73.2 us
  matrix products: 29.2 us -> 2.69 us
  local copies, waits for them, and re-layouts: 19.5 us -> 38.3 us
  other arithmetic: 23.5 us -> 10.4 us
    reduce_scatter x2 -> x0, waiting for transfers between devices: 164 us -> none  [the longest x1 110 us: fast_shards(): lax.psum_scatter(in_local, both, scatter_dimension=0, tiled=True)]
    all_gather x1 -> x0, blocking collectives: 109 us -> none  [fast_shards(): lax.all_gather(packed, both, axis=0, tiled=True)]
    all_to_all x8 -> x1, blocking collectives: 165 us -> 65.6 us  [exchange(): return lax.all_to_all(values, 'sp', split_axis=0, concat_axis=0, tiled=True)]
    pallas_call x3 -> x13, Pallas kernels: 39.1 us -> 88.4 us  [the longest x2 27.7 us: filter_forward(): pl.pallas_call(functools.partial(filter_body, pieces), name='filter_forwa...]
    ppermute x0 -> x17, waiting for transfers between devices: none -> 40.6 us  [swap(): lax.ppermute(values, axis, [(i, i ^ bit) for i in range(SIZES[axis])])]
    unnamed x1 -> x0, blocking collectives: 37.3 us -> none
    unnamed x6 -> x1, waiting for transfers between devices: 26.8 us -> 0.02 us
    dot_general x2, matrix products: 29.2 us -> 2.69 us  [spread_columns(): jnp.einsum(form, halves, jnp.asarray(pick[:, first:first + 2], BF16), pre...]
  transfers between devices with their start and end apart: 13 -> 27, of which waited for: 5 -> 13; matrix products, arithmetic and copies ran while one was open for 7% -> 7% of each run, Pallas kernels for 17% -> 40%
where the time goes in v2:
time: 502 us; the launch traced here: 495 us
  Pallas kernels  209 us (42%)
  waiting for transfers between devices  80.5 us (16%)
  starting transfers between devices  73.2 us (15%)
  blocking collectives  65.6 us (13%)
  local copies, waits for them, and re-layouts  38.3 us (8%)
  between operations  16.1 us (3%)
  other arithmetic  10.4 us (2%)
    pallas_call x3, Pallas kernels, dense(): pl.pallas_call(dense_body, name='dense_group', grid=(hidden // FCHUNK,),...  76.1 us
    all_to_all x1, blocking collectives, exchange(): return lax.all_to_all(values, 'sp', split_axis=0, concat_axis=0, tiled=True)  65.6 us
    all_to_all x9, starting transfers between devices, exchange(): return lax.all_to_all(values, 'sp', split_axis=0, concat_axis=0, tiled=True)  48.2 us
    ppermute x17, waiting for transfers between devices, swap(): lax.ppermute(values, axis, [(i, i ^ bit) for i in range(SIZES[axis])])  40.6 us
    all_to_all x9, waiting for transfers between devices, exchange(): return lax.all_to_all(values, 'sp', split_axis=0, concat_axis=0, tiled=True)  39.9 us
    pallas_call x2, Pallas kernels, filter_backward(): pl.pallas_call(functools.partial(filter_back_body, groups), name='filter_...  37.2 us
    pallas_call x2, Pallas kernels, filter_forward(): pl.pallas_call(functools.partial(filter_body, pieces), name='filter_forwa...  27.7 us
    ppermute x17, starting transfers between devices, swap(): lax.ppermute(values, axis, [(i, i ^ bit) for i in range(SIZES[axis])])  24.9 us
  transfers between devices with their start and end apart: 27, of which 13 were waited for; matrix products, arithmetic and copies ran while one was open for 7% of the time, Pallas kernels for 40%

profile of v2, /device:TPU:0, one launch (start us, length us, event | category | flops | bytes accessed | tf_op | source)
XLA Modules:
  0.0 495.4 jit_solution(10760906983884502989)
XLA Ops:
  8.5 7.1 %norm_and_longitude.1 = (bf16[8,17,16,384]{3,2,1,0:T(8,128)(2,1)}, bf16[8,15,16,384]{3,2,1,0:T(8,128)(2,1)}) custom-call(bf16[1,12,160,768]{3,2,1,0:T(8,128)(2,1)} %tokens_ref.9, bf16[640,640]{1,0:T(8,128)(2,1)} %constant.277.clone.table_ref, f32[24,384]{1,0:T(8,128)} %filter_ref.1, f32[1,384]{1,0:T(1,128)} %reshape.131.small_ref), custom_call_target="tpu_custom_call" | custom-call | flops 8049999872 | bytes 2949120 | tf_op jit(solution)/shard_map/norm_and_longitude/pallas_call | solution.py:435
  17.1 65.6 %all_to_all.50.refs_0_.refs_1_.refs_2_.refs_8_.refs_9_.refs_10_ = bf16[8,17,16,384]{3,2,1,0:T(8,128)(2,1)S(1)} all-to-all(bf16[8,17,16,384]{3,2,1,0:T(8,128)(2,1)S(1)} %copy-done.7), channel_id=1, replica_groups=mesh['y'=2,'core'=2,'sp'=8] {'sp'}, dimensions={0} | all-to-all | bytes 3342336 | tf_op jit(solution)/shard_map/all_to_all | solution.py:920
  88.8 4.3 all-to-all-start.1
  93.1 13.0 %collective-permute-done.1 = bf16[2,8,32,384]{3,2,1,0:T(8,128)(2,1)S(1)} collective-permute-done((bf16[2,8,32,384]{3,2,1,0:T(8,128)(2,1)S(1)}, bf16[2,8,32,384]{3,2,1,0:T(8,128)(2,1)S(1)}, u32[]{:S(2)}, u32[]{:S(2)}) %collective-permute-start.1) | collective-permute-done | bytes 393248 | tf_op jit(solution)/shard_map/ppermute | solution.py:929
  114.2 13.8 %filter_forward.2 = (bf16[8,3,5,16,384]{4,3,2,1,0:T(8,128)(2,1)}, bf16[5,416,384]{2,1,0:T(8,128)(2,1)}, bf16[5,2,208,768]{3,2,1,0:T(8,128)(2,1)}, bf16[5,4,208,384]{3,2,1,0:T(8,128)(2,1)}) custom-call(s32[5]{0:T(128)} %and_select_fusion.pick_ref, bf16[8,17,16,384]{3,2,1,0:T(8,128)(2,1)} %copy-done.6, bf16[8,17,16,384]{3,2,1,0:T(8,128)(2,1)} %copy-done.6, ...), custom_call_target="tpu_custom_call" | custom-call | flops 16099999744 | bytes 12582912 | tf_op jit(solution)/shard_map/filter_forward/pallas_call | solution.py:544
  128.1 14.8 %all-to-all-done.1.refs_0_.refs_1_.refs_2_.refs_8_.refs_9_.refs_10_ = bf16[8,15,16,384]{3,2,1,0:T(8,128)(2,1)} async-done(((bf16[8,15,16,384]{3,2,1,0:T(8,128)(2,1)}), bf16[8,15,16,384]{3,2,1,0:T(8,128)(2,1)}, u32[]{:S(2)}, u32[]{:S(2)}) %all-to-all-start.1) | async-done | bytes 1474592 | tf_op jit(solution)/shard_map/all_to_all | solution.py:920
  142.8 3.9 all-to-all-start.2
  146.7 13.9 %filter_forward.3 = (bf16[8,1,5,16,384]{4,3,2,1,0:T(8,128)(2,1)}, bf16[8,2,5,16,384]{4,3,2,1,0:T(8,128)(2,1)}, bf16[5,416,384]{2,1,0:T(8,128)(2,1)}, bf16[5,2,20...) custom-call(s32[5]{0:T(128)} %and_select_fusion.pick_ref, ...), custom_call_target="tpu_custom_call" | custom-call | flops 16099999744 | bytes 12582912 | tf_op jit(solution)/shard_map/filter_forward/pallas_call | solution.py:544
  160.6 6.6 %fusion.11 = (bf16[32,96,768]{2,1,0:T(8,128)(2,1)}, bf16[32,96,768]{2,1,0:T(8,128)(2,1)S(1)}) fusion(bf16[32,192,768]{2,1,0:T(8,128)(2,1)} %bitcast.81), kind=kLoop, calls=%fused_computation.68 | loop fusion | bytes 18874368 | tf_op jit(solution)/shard_map/slice | solution.py:1178
  172.8 9.1 %all-to-all-done.2.low_ref = bf16[8,3,5,16,384]{4,3,2,1,0:T(8,128)(2,1)S(1)} async-done(((bf16[8,3,5,16,384]{4,3,2,1,0:T(8,128)(2,1)}), bf16[8,3,5,16,384]{4,3,2,1,0:T(8,128)(2,1)S(1)}, u32[]{:S(2)}, u32[]{:S(2)}) %all-to-all-start.2) | async-done | bytes 1474592 | tf_op jit(solution)/shard_map/all_to_all | solution.py:920
  181.8 3.6 all-to-all-start.3
  186.2 13.2 %all-to-all-done.3.high_ref = bf16[8,1,5,16,384]{4,3,2,1,0:T(8,128)(2,1)S(1)} async-done(((bf16[8,1,5,16,384]{4,3,2,1,0:T(8,128)(2,1)}), bf16[8,1,5,16,384]{4,3,2,1,0:T(8,128)(2,1)S(1)}, u32[]{:S(2)}, u32[]{:S(2)}) %all-to-all-start.3) | async-done | bytes 491552 | tf_op jit(solution)/shard_map/all_to_all | solution.py:920
  199.4 4.0 all-to-all-start.4
  203.5 25.4 %dense_group.3 = (bf16[1,12,160,768]{3,2,1,0:T(8,128)(2,1)}, f32[1,12,160,768]{3,2,1,0:T(8,128)}, bf16[1920,768]{1,0:T(8,128)(2,1)}, bf16[1920,768]{1,0:T(8,128)...) custom-call(bf16[1,12,160,768]{3,2,1,0:T(8,128)(2,1)} %tokens_ref.9,, ...), custom_call_target="tpu_custom_call" | custom-call | flops 28750000128 | bytes 31457280 | tf_op jit(solution)/shard_map/dense_group/pallas_call | solution.py:801
  229.8 6.6 %all-to-all-start.5 = ((bf16[8,5,16,768]{3,2,1,0:T(8,128)(2,1)}), bf16[8,5,16,768]{3,2,1,0:T(8,128)(2,1)S(1)}, u32[]{:S(2)}, u32[]{:S(2)}) async-start(bf16[8,5,16,768]{3,2,1,0:T(8,128)(2,1)} %get-tuple-element.143), calls=%async_computation.5 | async-start | bytes 1966080 | tf_op jit(solution)/shard_map/all_to_all | solution.py:920
  236.4 25.4 %dense_group.4 = (bf16[1,12,160,768]{3,2,1,0:T(8,128)(2,1)}, f32[1,12,160,768]{3,2,1,0:T(8,128)}, bf16[1920,768]{1,0:T(8,128)(2,1)}, bf16[1920,768]{1,0:T(8,128)...) custom-call(bf16[1,12,160,768]{3,2,1,0:T(8,128)(2,1)} %tokens_ref.9,, ...), custom_call_target="tpu_custom_call", output_to_operand_aliasing={{0}: (10, {}), {1}: (11, {}), {2}: (12, {}), {3}: (13, {}),... | custom-call | flops 28750000128 | bytes 31457280 | tf_op jit(solution)/shard_map/dense_group/pallas_call | solution.py:801
  261.8 6.2 %all-to-all-start.6 = ((bf16[8,5,16,768]{3,2,1,0:T(8,128)(2,1)}), bf16[8,5,16,768]{3,2,1,0:T(8,128)(2,1)S(1)}, u32[]{:S(2)}, u32[]{:S(2)}) async-start(bf16[8,5,16,768]{3,2,1,0:T(8,128)(2,1)} %get-tuple-element.145), calls=%async_computation.6 | async-start | bytes 1966080 | tf_op jit(solution)/shard_map/all_to_all | solution.py:920
  268.0 25.4 %dense_group.5 = (bf16[1,12,160,768]{3,2,1,0:T(8,128)(2,1)}, f32[1,12,160,768]{3,2,1,0:T(8,128)}, bf16[1920,768]{1,0:T(8,128)(2,1)}, bf16[1920,768]{1,0:T(8,128)...) custom-call(bf16[1,12,160,768]{3,2,1,0:T(8,128)(2,1)} %tokens_ref.9,, ...), custom_call_target="tpu_custom_call", output_to_operand_aliasing={{0}: (10, {}), {1}: (11, {}), {2}: (12, {}), {3}: (13, {}),... | custom-call | flops 28750000128 | bytes 31457280 | tf_op jit(solution)/shard_map/dense_group/pallas_call | solution.py:801
  293.4 6.2 %all-to-all-start.7 = ((bf16[8,5,16,768]{3,2,1,0:T(8,128)(2,1)}), bf16[8,5,16,768]{3,2,1,0:T(8,128)(2,1)S(1)}, u32[]{:S(2)}, u32[]{:S(2)}) async-start(bf16[8,5,16,768]{3,2,1,0:T(8,128)(2,1)} %get-tuple-element.147), calls=%async_computation.7 | async-start | bytes 1966080 | tf_op jit(solution)/shard_map/all_to_all | solution.py:920
  299.7 14.9 %in_weight_grad.1 = (bf16[384,3072]{1,0:T(8,128)(2,1)}, bf16[384,3072]{1,0:T(8,128)(2,1)}) custom-call(s32[1]{0:T(128)} %bitcast.25.pick_ref, bf16[1920,768]{1,0:T(8,128)(2,1)} %get-tuple-element.159.second_ref, bf16[1920,3072]{1,0:T(8,128)(2,1)} %get-tuple-element.160.grad_pre_ref), custom_call_target="tpu_custom_call" | custom-call | flops 1048576 | bytes 1048576 | tf_op jit(solution)/shard_map/in_weight_grad/pallas_call | solution.py:999
  314.7 15.5 %out_weight_grad.1 = (bf16[2,2,384,768]{3,2,1,0:T(8,128)(2,1)}, bf16[2,2,384,768]{3,2,1,0:T(8,128)(2,1)}) custom-call(s32[1]{0:T(128)} %bitcast.25.pick_ref, bf16[1920,3072]{1,0:T(8,128)(2,1)} %get-tuple-element.155.act_ref, bf16[1920,768]{1,0:T(8,128)(2,1)} %get-tuple-element.156.grad_low_ref), custom_call_target="tpu_custom_call" | custom-call | flops 1048576 | bytes 1048576 | tf_op jit(solution)/shard_map/out_weight_grad/pallas_call | solution.py:1053
  331.5 18.5 %filter_backward.2 = (bf16[8,3,5,16,384]{4,3,2,1,0:T(8,128)(2,1)}, f32[384,768]{1,0:T(8,128)}, f32[768,384]{1,0:T(8,128)}, f32[8,384]{1,0:T(8,128)}) custom-call(s32[5]{0:T(128)} %and_select_fusion.pick_ref, bf16[8,5,16,768]{3,2,1,0:T(8,128)(2,1)} %copy-done.16, bf16[8,5,16,768]{3,2,1,0:T(8,128)(2,1)} %copy-done.17, bf16[8,5,16,768]{3,2,1,0:T(8,128)(2,1)} %copy-done.18, ...), custom_call_target="tpu_custom_call" | custom-call | flops 20700000256 | bytes 12582912 | tf_op jit(solution)/shard_map/filter_backward/pallas_call | solution.py:656
  350.0 6.0 %all-to-all-start.8 = ((bf16[8,3,5,16,384]{4,3,2,1,0:T(8,128)(2,1)}), bf16[8,3,5,16,384]{4,3,2,1,0:T(8,128)(2,1)}, u32[]{:S(2)}, u32[]{:S(2)}) async-start(bf16[8,3,5,16,384]{4,3,2,1,0:T(8,128)(2,1)} %get-tuple-element.152), calls=%async_computation.8 | async-start | bytes 2949120 | tf_op jit(solution)/shard_map/all_to_all | solution.py:920
  356.1 3.6 add_split.8
  362.7 3.5 add_split.9
  368.2 18.7 %filter_backward.3 = (bf16[8,3,5,16,384]{4,3,2,1,0:T(8,128)(2,1)}, f32[384,768]{1,0:T(8,128)}, f32[768,384]{1,0:T(8,128)}, f32[8,384]{1,0:T(8,128)}) custom-call(s32[5]{0:T(128)} %and_select_fusion.pick_ref, bf16[8,5,16,768]{3,2,1,0:T(8,128)(2,1)} %copy-done.16, bf16[8,5,16,768]{3,2,1,0:T(8,128)(2,1)} %copy-done.17, bf16[8,5,16,768]{3,2,1,0:T(8,128)(2,1)} %copy-done.18, ...), custom_call_target="tpu_custom_call" | custom-call | flops 20700000256 | bytes 12582912 | tf_op jit(solution)/shard_map/filter_backward/pallas_call | solution.py:656
  404.6 7.3 %all-to-all-start.9 = ((bf16[8,3,5,16,384]{4,3,2,1,0:T(8,128)(2,1)}), bf16[8,3,5,16,384]{4,3,2,1,0:T(8,128)(2,1)S(1)}, u32[]{:S(2)}, u32[]{:S(2)}) async-start(bf16[8,3,5,16,384]{4,3,2,1,0:T(8,128)(2,1)} %get-tuple-element.182), calls=%async_computation.9 | async-start | bytes 2949120 | tf_op jit(solution)/shard_map/all_to_all | solution.py:920
  423.9 6.4 %collective-permute-done.7 = f32[2,2,2,25,384]{4,2,3,1,0:T(2,128)} collective-permute-done((f32[2,2,2,25,384]{4,2,3,1,0:T(2,128)}, f32[2,2,2,25,384]{4,2,3,1,0:T(2,128)}, u32[]{:S(2)}, u32[]{:S(2)}) %collective-permute-start.7) | collective-permute-done | bytes 307232 | tf_op jit(solution)/shard_map/ppermute | solution.py:929
  433.9 10.5 %collective-permute-done.13.got_one.got_two = bf16[96,3072]{1,0:T(8,128)(2,1)S(1)} collective-permute-done((bf16[96,3072]{1,0:T(8,128)(2,1)}, bf16[96,3072]{1,0:T(8,128)(2,1)S(1)}, u32[]{:S(2)}, u32[]{:S(2)}) %collective-permute-start.13) | collective-permute-done | bytes 589856 | tf_op jit(solution)/shard_map/ppermute | solution.py:929
  447.3 3.4 collective-permute-start.14
  465.6 4.5 collective-permute-start.16
  473.4 10.2 %longitude_and_norm_grad.1 = f32[1,12,160,768]{3,2,1,0:T(8,128)} custom-call(bf16[1,12,160,768]{3,2,1,0:T(8,128)(2,1)} %tokens_ref.9, f32[1,12,160,768]{3,2,1,0:T(8,128)} %get-tuple-element.141.mixed_grad_ref, bf16[8,3,5,16,384]{4,3,2,1,0:T(8,128)(2,1)} %all-to-all-done.8.low_ref, bf16[8,3,5,16,384]{4,3,2,1,0:T(8,128)(2,1)} %copy-done.8, ...), custom_call_target="tpu_custom_call" | custom-call | flops 13799999488 | bytes 16777216 | tf_op jit(solution)/shard_map/longitude_and_norm_grad/pallas_call | solution.py:873
  (241 shorter events, 88.2 us)
Async XLA Ops:
  7.2 153.4 %all-gather.3.cloned.1.call-start = ((), (), s32[]{:S(2)}) async-start(), calls=%async_computation.10 | async-start | bytes 9732096 | tf_op jit(solution)/shard_map/all_gather | solution.py:1175
  83.9 1.8 collective-permute-start
  85.9 20.2 %collective-permute-start.1 = (bf16[2,8,32,384]{3,2,1,0:T(8,128)(2,1)S(1)}, bf16[2,8,32,384]{3,2,1,0:T(8,128)(2,1)S(1)}, u32[]{:S(2)}, u32[]{:S(2)}) collective-permute-start(bf16[2,8,32,384]{3,2,1,0:T(8,128)(2,1)S(1)} %pad_maximum_fusion.1), channel_id=1, source_target_pairs={{0,16},{16,0},{1,17},{17,1},{2,18},{18,2},{3,19},{19,3},{4,20},{20... | collective-permute-start | bytes 1179656 | tf_op jit(solution)/shard_map/ppermute | solution.py:929
  88.8 54.1 %all-to-all-start.1 = ((bf16[8,15,16,384]{3,2,1,0:T(8,128)(2,1)}), bf16[8,15,16,384]{3,2,1,0:T(8,128)(2,1)}, u32[]{:S(2)}, u32[]{:S(2)}) async-start(bf16[8,15,16,384]{3,2,1,0:T(8,128)(2,1)} %get-tuple-element.120), calls=%async_computation.1 | async-start | bytes 2949120 | tf_op jit(solution)/shard_map/all_to_all | solution.py:920
  142.8 39.0 %all-to-all-start.2 = ((bf16[8,3,5,16,384]{4,3,2,1,0:T(8,128)(2,1)}), bf16[8,3,5,16,384]{4,3,2,1,0:T(8,128)(2,1)S(1)}, u32[]{:S(2)}, u32[]{:S(2)}) async-start(bf16[8,3,5,16,384]{4,3,2,1,0:T(8,128)(2,1)} %get-tuple-element.121), calls=%async_computation.2 | async-start | bytes 2949120 | tf_op jit(solution)/shard_map/all_to_all | solution.py:920
  181.8 17.6 %copy-start.9 = (bf16[8,3,5,16,384]{4,3,2,1,0:T(8,128)(2,1)}, bf16[8,3,5,16,384]{4,3,2,1,0:T(8,128)(2,1)S(1)}, u32[]{:S(2)}) copy-start(bf16[8,3,5,16,384]{4,3,2,1,0:T(8,128)(2,1)S(1)} %all-to-all-done.2.low_ref) | copy-start | bytes 4423684
  181.8 17.6 %all-to-all-start.3 = ((bf16[8,1,5,16,384]{4,3,2,1,0:T(8,128)(2,1)}), bf16[8,1,5,16,384]{4,3,2,1,0:T(8,128)(2,1)S(1)}, u32[]{:S(2)}, u32[]{:S(2)}) async-start(bf16[8,1,5,16,384]{4,3,2,1,0:T(8,128)(2,1)} %get-tuple-element.126), calls=%async_computation.3 | async-start | bytes 983040 | tf_op jit(solution)/shard_map/all_to_all | solution.py:920
  199.4 29.4 %all-to-all-start.4 = ((bf16[8,2,5,16,384]{4,3,2,1,0:T(8,128)(2,1)}), bf16[8,2,5,16,384]{4,3,2,1,0:T(8,128)(2,1)S(1)}, u32[]{:S(2)}, u32[]{:S(2)}) async-start(bf16[8,2,5,16,384]{4,3,2,1,0:T(8,128)(2,1)} %get-tuple-element.127), calls=%async_computation.4 | async-start | bytes 1966080 | tf_op jit(solution)/shard_map/all_to_all | solution.py:920
  229.8 32.0 %all-to-all-start.5 = ((bf16[8,5,16,768]{3,2,1,0:T(8,128)(2,1)}), bf16[8,5,16,768]{3,2,1,0:T(8,128)(2,1)S(1)}, u32[]{:S(2)}, u32[]{:S(2)}) async-start(bf16[8,5,16,768]{3,2,1,0:T(8,128)(2,1)} %get-tuple-element.143), calls=%async_computation.5 | async-start | bytes 1966080 | tf_op jit(solution)/shard_map/all_to_all | solution.py:920
  261.8 31.6 %copy-start.16 = (bf16[8,5,16,768]{3,2,1,0:T(8,128)(2,1)}, bf16[8,5,16,768]{3,2,1,0:T(8,128)(2,1)S(1)}, u32[]{:S(2)}) copy-start(bf16[8,5,16,768]{3,2,1,0:T(8,128)(2,1)S(1)} %all-to-all-done.5.refs_0_) | copy-start | bytes 2949124
  261.8 31.6 %all-to-all-start.6 = ((bf16[8,5,16,768]{3,2,1,0:T(8,128)(2,1)}), bf16[8,5,16,768]{3,2,1,0:T(8,128)(2,1)S(1)}, u32[]{:S(2)}, u32[]{:S(2)}) async-start(bf16[8,5,16,768]{3,2,1,0:T(8,128)(2,1)} %get-tuple-element.145), calls=%async_computation.6 | async-start | bytes 1966080 | tf_op jit(solution)/shard_map/all_to_all | solution.py:920
  293.4 21.2 %copy-start.17 = (bf16[8,5,16,768]{3,2,1,0:T(8,128)(2,1)}, bf16[8,5,16,768]{3,2,1,0:T(8,128)(2,1)S(1)}, u32[]{:S(2)}) copy-start(bf16[8,5,16,768]{3,2,1,0:T(8,128)(2,1)S(1)} %all-to-all-done.6.refs_1_) | copy-start | bytes 2949124
  293.4 36.7 %all-to-all-start.7 = ((bf16[8,5,16,768]{3,2,1,0:T(8,128)(2,1)}), bf16[8,5,16,768]{3,2,1,0:T(8,128)(2,1)S(1)}, u32[]{:S(2)}, u32[]{:S(2)}) async-start(bf16[8,5,16,768]{3,2,1,0:T(8,128)(2,1)} %get-tuple-element.147), calls=%async_computation.7 | async-start | bytes 1966080 | tf_op jit(solution)/shard_map/all_to_all | solution.py:920
  314.6 16.2 %copy-start.54 = (f32[8,768]{1,0:T(8,128)S(1)}, f32[8,768]{1,0:T(8,128)}, u32[]{:S(2)}) copy-start(f32[8,768]{1,0:T(8,128)} %get-tuple-element.191) | copy-start | bytes 73732
  330.2 25.9 %collective-permute-start.2 = (bf16[384,3072]{1,0:T(8,128)(2,1)}, bf16[384,3072]{1,0:T(8,128)(2,1)}, u32[]{:S(2)}, u32[]{:S(2)}) collective-permute-start(bf16[384,3072]{1,0:T(8,128)(2,1)} %get-tuple-element.164), channel_id=1, source_target_pairs={{0,8},{8,0},{1,9},{9,1},{2,10},{10,2},{3,11},{11,3},{4,12},{12,4},... | collective-permute-start | bytes 7077896 | tf_op jit(solution)/shard_map/ppermute | solution.py:929
  330.2 31.0 %collective-permute-start.3 = (bf16[1536,768]{1,0:T(8,128)(2,1)}, bf16[1536,768]{1,0:T(8,128)(2,1)S(1)}, u32[]{:S(2)}, u32[]{:S(2)}) collective-permute-start(bf16[1536,768]{1,0:T(8,128)(2,1)} %bitcast.109), channel_id=1, source_target_pairs={{0,8},{8,0},{1,9},{9,1},{2,10},{10,2},{3,11},{11,3},{4,12},{12,4},... | collective-permute-start | bytes 7077896 | tf_op jit(solution)/shard_map/ppermute | solution.py:929
  350.0 41.3 %all-to-all-start.8 = ((bf16[8,3,5,16,384]{4,3,2,1,0:T(8,128)(2,1)}), bf16[8,3,5,16,384]{4,3,2,1,0:T(8,128)(2,1)}, u32[]{:S(2)}, u32[]{:S(2)}) async-start(bf16[8,3,5,16,384]{4,3,2,1,0:T(8,128)(2,1)} %get-tuple-element.152), calls=%async_computation.8 | async-start | bytes 2949120 | tf_op jit(solution)/shard_map/all_to_all | solution.py:920
  359.7 35.5 %collective-permute-start.5 = (bf16[192,3072]{1,0:T(8,128)(2,1)}, bf16[192,3072]{1,0:T(8,128)(2,1)S(1)}, u32[]{:S(2)}, u32[]{:S(2)}) collective-permute-start(bf16[192,3072]{1,0:T(8,128)(2,1)} %get-tuple-element.166), channel_id=1, source_target_pairs={{0,16},{16,0},{1,17},{17,1},{2,18},{18,2},{3,19},{19,3},{4,20},{20... | collective-permute-start | bytes 3538952 | tf_op jit(solution)/shard_map/ppermute | solution.py:929
  366.2 34.6 %collective-permute-start.4 = (bf16[768,768]{1,0:T(8,128)(2,1)}, bf16[768,768]{1,0:T(8,128)(2,1)S(1)}, u32[]{:S(2)}, u32[]{:S(2)}) collective-permute-start(bf16[768,768]{1,0:T(8,128)(2,1)} %get-tuple-element.170), channel_id=1, source_target_pairs={{0,1},{1,0},{2,3},{3,2},{4,5},{5,4},{6,7},{7,6},{8,9},{9,8},{10,11... | collective-permute-start | bytes 3538952 | tf_op jit(solution)/shard_map/ppermute | solution.py:929
  368.2 19.4 %copy-start.49 = (f32[8,768]{1,0:T(8,128)S(1)}, f32[8,768]{1,0:T(8,128)}, u32[]{:S(2)}) copy-start(f32[8,768]{1,0:T(8,128)} %copy-done.48) | copy-start | bytes 73732
  404.6 49.2 %all-to-all-start.9 = ((bf16[8,3,5,16,384]{4,3,2,1,0:T(8,128)(2,1)}), bf16[8,3,5,16,384]{4,3,2,1,0:T(8,128)(2,1)S(1)}, u32[]{:S(2)}, u32[]{:S(2)}) async-start(bf16[8,3,5,16,384]{4,3,2,1,0:T(8,128)(2,1)} %get-tuple-element.182), calls=%async_computation.9 | async-start | bytes 2949120 | tf_op jit(solution)/shard_map/all_to_all | solution.py:920
  414.3 2.2 collective-permute-start.6
  419.9 10.4 %collective-permute-start.7 = (f32[2,2,2,25,384]{4,2,3,1,0:T(2,128)}, f32[2,2,2,25,384]{4,2,3,1,0:T(2,128)}, u32[]{:S(2)}, u32[]{:S(2)}) collective-permute-start(f32[2,2,2,25,384]{4,2,3,1,0:T(2,128)} %dynamic-slice_bitcast_fusion), channel_id=1, source_target_pairs={{0,16},{16,0},{1,17},{17,1},{2,18},{18,2},{3,19},{19,3},{4,20},{20... | collective-permute-start | bytes 921608 | tf_op jit(solution)/shard_map/ppermute | solution.py:929
  421.4 23.0 %collective-permute-start.13 = (bf16[96,3072]{1,0:T(8,128)(2,1)}, bf16[96,3072]{1,0:T(8,128)(2,1)S(1)}, u32[]{:S(2)}, u32[]{:S(2)}) collective-permute-start(bf16[96,3072]{1,0:T(8,128)(2,1)} %get-tuple-element.181), channel_id=1, source_target_pairs={{0,1},{1,0},{2,3},{3,2},{4,5},{5,4},{6,7},{7,6},{8,9},{9,8},{10,11... | collective-permute-start | bytes 1769480 | tf_op jit(solution)/shard_map/ppermute | solution.py:929
  423.4 27.3 %collective-permute-start.11 = (bf16[384,768]{1,0:T(8,128)(2,1)}, bf16[384,768]{1,0:T(8,128)(2,1)S(1)}, u32[]{:S(2)}, u32[]{:S(2)}) collective-permute-start(bf16[384,768]{1,0:T(8,128)(2,1)} %get-tuple-element.179), channel_id=1, source_target_pairs={{0,16},{16,0},{1,17},{17,1},{2,18},{18,2},{3,19},{19,3},{4,20},{20... | collective-permute-start | bytes 1769480 | tf_op jit(solution)/shard_map/ppermute | solution.py:929
  431.8 21.8 %collective-permute-start.8 = (f32[2,2,25,384]{3,1,2,0:T(2,128)S(1)}, f32[2,2,25,384]{3,1,2,0:T(2,128)S(1)}, u32[]{:S(2)}, u32[]{:S(2)}) collective-permute-start(f32[2,2,25,384]{3,1,2,0:T(2,128)S(1)} %bitcast.103), channel_id=1, source_target_pairs={{0,1},{1,0},{2,3},{3,2},{4,5},{5,4},{6,7},{7,6},{8,9},{9,8},{10,11... | collective-permute-start | bytes 460808 | tf_op jit(solution)/shard_map/ppermute | solution.py:929
  447.3 11.1 %collective-permute-start.14 = (bf16[48,3072]{1,0:T(8,128)(2,1)}, bf16[48,3072]{1,0:T(8,128)(2,1)S(1)}, u32[]{:S(2)}, u32[]{:S(2)}) collective-permute-start(bf16[48,3072]{1,0:T(8,128)(2,1)} %get-tuple-element.205), channel_id=1, source_target_pairs={{0,2},{1,3},{2,0},{3,1},{4,6},{5,7},{6,4},{7,5},{8,10},{9,11},{10,... | collective-permute-start | bytes 884744 | tf_op jit(solution)/shard_map/ppermute | solution.py:929
  453.6 9.5 %collective-permute-start.12 = (bf16[192,768]{1,0:T(8,128)(2,1)}, bf16[192,768]{1,0:T(8,128)(2,1)S(1)}, u32[]{:S(2)}, u32[]{:S(2)}) collective-permute-start(bf16[192,768]{1,0:T(8,128)(2,1)} %get-tuple-element.201), channel_id=1, source_target_pairs={{0,2},{1,3},{2,0},{3,1},{4,6},{5,7},{6,4},{7,5},{8,10},{9,11},{10,... | collective-permute-start | bytes 884744 | tf_op jit(solution)/shard_map/ppermute | solution.py:929
  453.9 16.3 %collective-permute-start.9 = (f32[2,25,384]{2,0,1:T(2,128)S(1)}, f32[2,25,384]{2,0,1:T(2,128)S(1)}, u32[]{:S(2)}, u32[]{:S(2)}) collective-permute-start(f32[2,25,384]{2,0,1:T(2,128)S(1)} %bitcast.104), channel_id=1, source_target_pairs={{0,2},{1,3},{2,0},{3,1},{4,6},{5,7},{6,4},{7,5},{8,10},{9,11},{10,... | collective-permute-start | bytes 230408 | tf_op jit(solution)/shard_map/ppermute | solution.py:929
  465.6 19.8 %collective-permute-start.16 = (bf16[96,768]{1,0:T(8,128)(2,1)}, bf16[96,768]{1,0:T(8,128)(2,1)S(1)}, u32[]{:S(2)}, u32[]{:S(2)}) collective-permute-start(bf16[96,768]{1,0:T(8,128)(2,1)} %get-tuple-element.211), channel_id=1, source_target_pairs={{0,4},{1,5},{2,6},{3,7},{4,0},{5,1},{6,2},{7,3},{8,12},{9,13},{10,... | collective-permute-start | bytes 442376 | tf_op jit(solution)/shard_map/ppermute | solution.py:929
  470.1 16.5 %collective-permute-start.15 = (bf16[24,3072]{1,0:T(8,128)(2,1)S(1)}, bf16[24,3072]{1,0:T(8,128)(2,1)S(1)}, u32[]{:S(2)}, u32[]{:S(2)}) collective-permute-start(bf16[24,3072]{1,0:T(8,128)(2,1)S(1)} %copy-done.66), channel_id=1, source_target_pairs={{0,4},{1,5},{2,6},{3,7},{4,0},{5,1},{6,2},{7,3},{8,12},{9,13},{10,... | collective-permute-start | bytes 442376 | tf_op jit(solution)/shard_map/ppermute | solution.py:929
  470.4 13.5 %collective-permute-start.10 = (f32[25,384]{1,0:T(8,128)S(1)}, f32[25,384]{1,0:T(8,128)S(1)}, u32[]{:S(2)}, u32[]{:S(2)}) collective-permute-start(f32[25,384]{1,0:T(8,128)S(1)} %bitcast.105), channel_id=1, source_target_pairs={{0,4},{1,5},{2,6},{3,7},{4,0},{5,1},{6,2},{7,3},{8,12},{9,13},{10,... | collective-permute-start | bytes 115208 | tf_op jit(solution)/shard_map/ppermute | solution.py:929
  (62 other events, 420.2 us)
Sparse Core Ops, SparseCore 0:
  16.5 124.1 all-gather.2
